TPU v7x, 32 devices: a whole 2x2x4 slice. The times are simulated.
32 devices in a mesh: seq: 8 (over z, y), own: 4 (over x, core).
Axes of the slice: x: 2, y: 2, z: 4, core: 2. Of those that a mesh axis runs over, the one named last changes fastest.
Arguments:
- inputs: bfloat16 [24576, 768], P(('seq', 'own')), may hold values from -30 to 30
- cotangent: bfloat16 [12288, 768], P(('seq', 'own')), may hold values from -30 to 30
- small_params: float32 [6, 768], replicated, may hold values from -2 to 2
- small_first: float32 [6, 768], replicated, may hold values from -1 to 1
- small_second: float32 [6, 768], replicated, may hold values from 0 to 0.01
- slot_of_matrix: int32 [7], replicated, may hold values from 0 to 7, as said below
- master: float32 [8, 768, 768], P('own'), may hold values from -3 to 3
- first_moment: float32 [8, 768, 768], P('own'), may hold values from -1 to 1
- second_moment: float32 [8, 768, 768], P('own'), may hold values from 0 to 0.01
- left_basis: float32 [8, 768, 768], P('own'), may hold values from -1 to 1, as said below
- right_basis: float32 [8, 768, 768], P('own'), may hold values from -1 to 1, as said below
Outputs:
- pooled: bfloat16 [12288, 768], P(('seq', 'own'))
- input_grad: bfloat16 [24576, 768], P(('seq', 'own'))
- grad_norm: float32 [], replicated
- new_master: float32 [8, 768, 768], P('own')
- new_first: float32 [8, 768, 768], P('own')
- new_second: float32 [8, 768, 768], P('own')
- new_small: float32 [6, 768], replicated
- new_small_first: float32 [6, 768], replicated
- new_small_second: float32 [6, 768], replicated
Inputs may be any that keep to these rules, and one draw needn't show every extreme that they name: `slot_of_matrix`: 7 distinct slot numbers; slot s lies on index s // 2 of own, no index of own holds more than 2 matrices and some index holds exactly 2. `left_basis`: each slot's matrix is orthogonal. `right_basis`: each slot's matrix is orthogonal.
All inputs are finite; a program needn't handle non-finite values.
Results may differ from a plain program's by a relative error of at most 0.011.
Values may be sent and summed in bfloat16 or wider, within the bound.
A program may use at most 192 MiB of HBM per device.

v0:
```python
import math

import jax
import jax.numpy as jnp
from jax import lax
from jax.sharding import PartitionSpec as P

NMAT = 7
STEP = 10


NORM_EPS = 1e-05
BETA_ONE = 0.9
BETA_TWO = 0.999
ADAM_EPS = 1e-08
DECAY_RATE = 0.01
LEARN_RATE = 0.02
SMALL_RATE = 0.1
CLIP_RATIO = 0.5
HIGHEST_PREC = lax.Precision.HIGHEST


def with_halo(value, sides, width):
    for axis, dim in sides:
        size, length = (lax.axis_size(axis), value.shape[dim])
        up = [(i, (i + 1) % size) for i in range(size - 1)]
        down = [(j, i) for i, j in up]
        last = lax.slice_in_dim(value, length - width, length, axis=dim)
        initial = lax.slice_in_dim(value, 0, width, axis=dim)
        before = lax.ppermute(last, axis, up)
        after = lax.ppermute(initial, axis, down)
        value = jnp.concatenate([before, value, after], axis=dim)
    return value


def gelu_smooth(values):
    return jax.nn.gelu(values, approximate=True)


def gelu_back(values, incoming):
    return jax.vjp(gelu_smooth, values)[1](incoming)[0]


def adam_moments(grads, first_old, second_old):
    first_new = BETA_ONE * first_old + (1.0 - BETA_ONE) * grads
    second_new = BETA_TWO * second_old + (1.0 - BETA_TWO) * grads * grads
    direction = (
        first_new
        / (1.0 - BETA_ONE**STEP)
        / (jnp.sqrt(second_new / (1.0 - BETA_TWO**STEP)) + ADAM_EPS)
    )
    return (first_new, second_new, direction)


def batch_stats(values, row_total):
    summed, squared = lax.psum(
        (jnp.sum(values, axis=0), jnp.sum(values * values, axis=0)), ("seq", "own")
    )
    mean_value = summed / row_total
    spread = squared / row_total - mean_value * mean_value
    return (mean_value, lax.rsqrt(spread + NORM_EPS))


def back_sums(grad_normed, normed, carried):
    return lax.psum(
        (
            jnp.sum(grad_normed, axis=0),
            jnp.sum(grad_normed * normed, axis=0),
            jnp.sum(carried, axis=0),
        ),
        ("seq", "own"),
    )


def per_device(
    inputs,
    cotangent,
    small_params,
    small_first,
    small_second,
    slot_of_matrix,
    master,
    first_moment,
    second_moment,
    left_basis,
    right_basis,
):
    positions, channels = inputs.shape
    own_count = lax.axis_size("own")
    row_total = positions * lax.axis_size("seq") * own_count
    capacity = master.shape[0]
    gathered = lax.all_gather(master.astype(jnp.bfloat16), "own", axis=0, tiled=True)
    weights = jnp.take(gathered, slot_of_matrix, axis=0)
    values = inputs.astype(jnp.float32)
    mean_one, rstd_one = batch_stats(values, row_total)
    normed_one = (values - mean_one) * rstd_one
    pre_one = normed_one * small_params[0] + small_params[1]
    active_one = gelu_smooth(pre_one).astype(jnp.bfloat16)
    padded = with_halo(active_one, ((("seq", "own"), 0),), 2)
    conv_out = jnp.zeros((positions, channels), jnp.float32)
    for offset in range(5):
        conv_out = conv_out + jnp.dot(
            padded[offset : offset + positions], weights[offset], preferred_element_type=jnp.float32
        )
    hidden = conv_out + small_params[2]
    mean_two, rstd_two = batch_stats(hidden, row_total)
    normed_two = (hidden - mean_two) * rstd_two
    pre_two = normed_two * small_params[3] + small_params[4]
    active_two = gelu_smooth(pre_two).astype(jnp.bfloat16)
    residual = (
        hidden
        + jnp.dot(active_two, weights[5], preferred_element_type=jnp.float32)
        + small_params[5]
    )
    residual_low = residual.astype(jnp.bfloat16)
    logits = jnp.dot(residual_low, weights[6], preferred_element_type=jnp.float32)
    pair_prob = jax.nn.softmax(logits.reshape(positions // 2, 2, channels), axis=1)
    residual_pairs = residual.reshape(positions // 2, 2, channels)
    pooled = jnp.sum(pair_prob * residual_pairs, axis=1).astype(jnp.bfloat16)
    incoming = cotangent.astype(jnp.float32)[:, None, :]
    grad_prob = incoming * residual_pairs
    grad_logits = pair_prob * (grad_prob - jnp.sum(pair_prob * grad_prob, axis=1, keepdims=True))
    grad_logits = grad_logits.reshape(positions, channels).astype(jnp.bfloat16)
    grad_pool = jnp.einsum(
        "lc,ld->cd", residual_low, grad_logits, preferred_element_type=jnp.float32
    )
    grad_resid = (pair_prob * incoming).reshape(positions, channels) + jnp.einsum(
        "ld,cd->lc", grad_logits, weights[6], preferred_element_type=jnp.float32
    )
    grad_branch_low = grad_resid.astype(jnp.bfloat16)
    grad_mix = jnp.einsum(
        "lc,ld->cd", active_two, grad_branch_low, preferred_element_type=jnp.float32
    )
    grad_active_two = jnp.einsum(
        "ld,cd->lc", grad_branch_low, weights[5], preferred_element_type=jnp.float32
    )
    grad_pre_two = gelu_back(pre_two, grad_active_two)
    sum_pre_two, sum_cross_two, sum_resid = back_sums(grad_pre_two, normed_two, grad_resid)
    grad_hidden = grad_resid + rstd_two * small_params[3] * (
        grad_pre_two - sum_pre_two / row_total - normed_two * sum_cross_two / row_total
    )
    grad_conv_low = grad_hidden.astype(jnp.bfloat16)
    grad_padded = with_halo(grad_conv_low, ((("seq", "own"), 0),), 2)
    grad_active_one = jnp.zeros((positions, channels), jnp.float32)
    tap_grads = []
    for offset in range(5):
        grad_active_one = grad_active_one + jnp.einsum(
            "ld,cd->lc",
            grad_padded[4 - offset : 4 - offset + positions],
            weights[offset],
            preferred_element_type=jnp.float32,
        )
        tap_grads.append(
            jnp.einsum(
                "lc,ld->cd",
                padded[offset : offset + positions],
                grad_conv_low,
                preferred_element_type=jnp.float32,
            )
        )
    grad_pre_one = gelu_back(pre_one, grad_active_one)
    sum_pre_one, sum_cross_one, sum_hidden = back_sums(grad_pre_one, normed_one, grad_hidden)
    input_grad = (
        rstd_one
        * small_params[0]
        * (grad_pre_one - sum_pre_one / row_total - normed_one * sum_cross_one / row_total)
    ).astype(jnp.bfloat16)
    small_grad = jnp.stack(
        [sum_cross_one, sum_pre_one, sum_hidden, sum_cross_two, sum_pre_two, sum_resid]
    )
    local_grads = jnp.stack(tap_grads + [grad_mix, grad_pool])
    slot_total = capacity * own_count
    summed_all = lax.psum(local_grads.astype(jnp.bfloat16), "seq").astype(jnp.float32)
    placed = (
        jnp.zeros((slot_total, channels, channels), jnp.float32).at[slot_of_matrix].set(summed_all)
    )
    owned = lax.psum_scatter(
        placed.astype(jnp.bfloat16), "own", scatter_dimension=0, tiled=True
    ).astype(jnp.float32)
    matrix_squares = lax.psum(jnp.sum(owned * owned), "own")
    grad_norm = jnp.sqrt(matrix_squares + jnp.sum(small_grad * small_grad))
    factor = jnp.minimum(1.0, CLIP_RATIO * channels * math.sqrt(NMAT) / (grad_norm + 1e-06))
    turned = jnp.einsum("kji,kjl->kil", left_basis, owned * factor, precision=HIGHEST_PREC)
    turned = jnp.einsum("kil,klm->kim", turned, right_basis, precision=HIGHEST_PREC)
    first_new, second_new, direction = adam_moments(turned, first_moment, second_moment)
    back_turn = jnp.einsum("kij,kjl->kil", left_basis, direction, precision=HIGHEST_PREC)
    back_turn = jnp.einsum("kil,kml->kim", back_turn, right_basis, precision=HIGHEST_PREC)
    master_new = master - LEARN_RATE * (back_turn + DECAY_RATE * master)
    slot_ids = lax.axis_index("own") * capacity + jnp.arange(capacity, dtype=jnp.int32)
    is_used = jnp.any(slot_ids[:, None] == slot_of_matrix[None, :], axis=1)[:, None, None]
    new_master = jnp.where(is_used, master_new, master)
    new_first = jnp.where(is_used, first_new, first_moment)
    new_second = jnp.where(is_used, second_new, second_moment)
    small_first_new, small_second_new, small_dir = adam_moments(
        small_grad * factor, small_first, small_second
    )
    new_small = small_params - SMALL_RATE * (small_dir + DECAY_RATE * small_params)
    return (
        pooled,
        input_grad,
        grad_norm,
        new_master,
        new_first,
        new_second,
        new_small,
        small_first_new,
        small_second_new,
    )


def solution(mesh):
    in_specs = (
        P(("seq", "own"), None),
        P(("seq", "own"), None),
        P(),
        P(),
        P(),
        P(),
        P("own", None, None),
        P("own", None, None),
        P("own", None, None),
        P("own", None, None),
        P("own", None, None),
    )
    out_specs = (
        P(("seq", "own"), None),
        P(("seq", "own"), None),
        P(),
        P("own", None, None),
        P("own", None, None),
        P("own", None, None),
        P(),
        P(),
        P(),
    )
    return jax.shard_map(
        per_device, mesh=mesh, in_specs=in_specs, out_specs=out_specs, check_vma=False
    )
```

profile of v0, /device:TPU:0, one launch (start us, length us, event | category | flops | bytes accessed | tf_op | source)
XLA Modules:
  0.0 747.8 jit_solution(17393326286503203876)
XLA Ops:
  7.2 4.0 convert_element_type.49
  11.3 1.2 copy-done.2
  12.8 42.5 %all-reduce.3 = (f32[768]{0:T(1024)S(1)}, f32[768]{0:T(1024)S(1)}) all-reduce(f32[768]{0:T(1024)S(1)} %get-tuple-element.18, f32[768]{0:T(1024)S(1)} %get-tuple-element.17), channel_id=1, replica_groups=mesh['seq'=8,'own'=4] {'seq','own'}, use_global_device_ids=true, to_apply=%region_3.4 | all-reduce | flops 1536 | bytes 12288 | tf_op jit(solution)/shard_map/psum | solution.py:56
  55.3 0.6 slice_reduce_fusion.2
  56.0 0.6 fusion.93
  56.6 1.1 fusion.33
  57.7 1.3 collective-permute-start.1
  59.0 3.0 collective-permute-start
  62.1 1.1 convert_element_type.53
  63.3 16.0 %all-gather.2.cloned.1.call-done = bf16[8,768,768]{2,1,0:T(8,128)(2,1)} async-done(((bf16[2,768,768]{2,1,0:T(8,128)(2,1)}), bf16[8,768,768]{2,1,0:T(8,128)(2,1)}) %all-gather.2.cloned.1.call-update) | async-done | bytes 9437200 | tf_op jit(solution)/shard_map/all_gather | solution.py:92
  79.3 8.4 %gather_fusion = bf16[7,768,768]{2,1,0:T(8,128)(2,1)} fusion(bf16[8,768,768]{2,1,0:T(8,128)(2,1)} %all-gather.2.cloned.1.call-done, s32[1024]{0:T(1024)S(1)} %pad_clamp_fusion), kind=kCustom, calls=%fused_computation | custom fusion | bytes 16515100 | tf_op jit(solution)/shard_map/jit(_take)/gather | solution.py:93
  87.7 7.4 broadcast_select_fusion
  95.1 2.3 fusion.83
  97.5 2.4 fusion.80
  99.9 2.4 fusion.81
  102.3 2.4 fusion.84
  104.7 3.6 fusion.115
  108.3 39.9 %all-reduce.2 = (f32[768]{0:T(1024)}, f32[768]{0:T(1024)}) all-reduce(f32[768]{0:T(1024)} %get-tuple-element.16, f32[768]{0:T(1024)S(1)} %get-tuple-element.15), channel_id=1, replica_groups=mesh['seq'=8,'own'=4] {'seq','own'}, use_global_device_ids=true, to_apply=%region_7.8 | all-reduce | flops 1536 | bytes 12288 | tf_op jit(solution)/shard_map/psum | solution.py:56
  148.2 1.3 fusion.92
  149.5 5.0 fusion.121
  154.5 2.9 dot_general.83
  157.4 4.9 fusion.122
  162.2 3.0 reshape.54
  165.3 2.7 fusion.49
  168.3 2.0 broadcast_multiply_fusion
  170.3 3.2 copy.48
  173.5 4.1 reshape.55
  177.6 3.4 multiply_reduce_fusion.1
  181.6 2.2 copy.50
  183.8 3.3 convert_element_type.55
  187.2 2.5 convolution_add_fusion
  189.8 6.5 fusion.114
  196.4 41.6 %all-reduce.1 = (f32[768]{0:T(1024)}, f32[768]{0:T(1024)S(1)}) all-reduce(f32[768]{0:T(1024)} %get-tuple-element.14, f32[768]{0:T(1024)} %get-tuple-element.13), channel_id=1, replica_groups=mesh['seq'=8,'own'=4] {'seq','own'}, use_global_device_ids=true, to_apply=%region_15.16 | all-reduce | flops 1536 | bytes 12288 | tf_op jit(solution)/shard_map/psum | solution.py:65
  238.5 3.9 fusion.117
  242.4 2.2 fusion.51
  244.7 2.1 fusion.53
  246.8 2.2 fusion.55
  249.0 2.2 fusion.57
  251.2 2.2 fusion.59
  253.4 2.8 fusion.61
  256.2 2.2 fusion.63
  258.6 266.0 %all-reduce.6.cloned.1.call-done = bf16[7,768,768]{2,1,0:T(8,128)(2,1)} async-done(((bf16[7,768,768]{2,1,0:T(8,128)(2,1)}), bf16[7,768,768]{2,1,0:T(8,128)(2,1)}) %all-reduce.6.cloned.1.call-update) | async-done | bytes 8257552 | tf_op jit(solution)/shard_map/psum | solution.py:173
  524.6 10.5 %convert_element_type.59 = f32[7,768,768]{2,1,0:T(8,128)} convert(bf16[7,768,768]{2,1,0:T(8,128)(2,1)} %all-reduce.6.cloned.1.call-done) | non-fusion elementwise | flops 4128768 | bytes 24772608 | tf_op jit(solution)/shard_map/convert_element_type | solution.py:173
  535.1 8.1 %broadcast_in_dim.54 = f32[8,768,768]{2,1,0:T(8,128)} broadcast(f32[]{:T(128)} %constant.28.clone.1), dimensions={} | broadcast | bytes 18874372 | tf_op jit(solution)/shard_map/broadcast_in_dim | solution.py:175
  543.2 28.3 %scatter_fusion = f32[8,768,768]{2,1,0:T(8,128)} fusion(f32[8,768,768]{2,1,0:T(8,128)} %broadcast_in_dim.54, s32[7]{0:T(128)S(1)} %copy-done.41, f32[7,768,768]{2,1,0:T(8,128)} %convert_element_type.59), kind=kCustom, calls=%fused_computation.1 | custom fusion | bytes 49545244 | tf_op jit(solution)/shard_map/scatter | solution.py:175
  571.5 9.8 %convert_element_type.60 = bf16[8,768,768]{2,1,0:T(8,128)(2,1)} convert(f32[8,768,768]{2,1,0:T(8,128)} %scatter_fusion) | non-fusion elementwise | flops 4718592 | bytes 28311552 | tf_op jit(solution)/shard_map/convert_element_type | solution.py:178
  581.3 0.6 copy-done.45
  582.6 1.3 collective-permute-start.2
  583.9 2.4 fusion.82
  586.4 3.2 collective-permute-start.3
  589.6 2.7 fusion.68
  592.3 2.7 fusion.74
  595.0 2.6 fusion.65
  597.6 5.5 fusion.113
  603.2 41.2 %all-reduce = (f32[768]{0:T(1024)S(1)}, f32[768]{0:T(1024)S(1)}, f32[1,768]{1,0:T(1,128)S(1)}, f32[1,768]{1,0:T(1,128)S(1)}) all-reduce(f32[768]{0:T(1024)S(1)} %get-tuple-element.12, f32[768]{0:T(1024)S(1)} %get-tuple-element.11, f32[1,768]{1,0:T(1,128)S(1)} %stack.58, ...), channel_id=1, replica_groups=mesh['seq'=8,'own'=4] {'seq','own'}, use_global_device_ids=true, to_apply=%region_19.20 | all-reduce | flops 3072 | bytes 24576 | tf_op jit(solution)/shard_map/psum | solution.py:65
  644.4 3.4 fusion.38
  647.8 12.6 %reduce-scatter.2.cloned.1.call-done = bf16[2,768,768]{2,1,0:T(8,128)(2,1)} async-done(((bf16[8,768,768]{2,1,0:T(8,128)(2,1)}), bf16[2,768,768]{2,1,0:T(8,128)(2,1)}) %reduce-scatter.2.cloned.1.call-update) | async-done | bytes 2359312 | tf_op jit(solution)/shard_map/reduce_scatter | solution.py:177
  660.4 3.6 fusion
  664.6 6.6 psum.93
  672.6 14.7 %fusion.1 = f32[2,768,768]{1,2,0:T(8,128)S(1)} fusion(f32[2,768,768]{2,1,0:T(8,128)} %param.20, bf16[2,768,768]{2,1,0:T(8,128)(2,1)S(1)} %copy-done.8, f32[]{:T(128)S(6)} %min.3), kind=kOutput, calls=%fused_computation.8 | convolution fusion | flops 10873995264 | bytes 11796484 | tf_op jit(solution)/shard_map/kji,kjl->kil/dot_general | solution.py:183
  687.3 17.9 %fusion.10 = (f32[2,768,768]{2,1,0:T(8,128)}, f32[2,768,768]{2,1,0:T(8,128)}, f32[2,768,768]{2,1,0:T(8,128)}) fusion(f32[2,768,768]{2,1,0:T(8,128)} %param.19, pred[2]{0:T(512)(128)(4,1)S(1)} %compare_reduce_fusion, f32[2,768,768]{2,1,0:T(8,128)} %param.18, f32[2,768,768]{1,2,0:T(8,128)S(1)} %fusion.1, f32[2,768,768]{2,1,0:T(8,128)S(1)} %bitcast.90), kind=kOutput, calls=%fused_computation.18 | convolution fusion | flops 10882252800 | bytes 33030146 | tf_op jit(solution)/shard_map/kil,klm->kim/dot_general | solution.py:184
  705.2 19.6 %fusion.3 = f32[2,768,768]{1,2,0:T(8,128)S(1)} fusion(f32[2,768,768]{2,1,0:T(8,128)} %param.20, f32[2,768,768]{2,1,0:T(8,128)} %get-tuple-element.62, f32[2,768,768]{2,1,0:T(8,128)} %param.18, f32[2,768,768]{2,1,0:T(8,128)} %param.19), kind=kOutput, calls=%fused_computation.10 | convolution fusion | flops 10884612096 | bytes 23592960 | tf_op jit(solution)/shard_map/kij,kjl->kil/dot_general | solution.py:186
  724.9 14.1 %subtract_select_fusion = f32[2,768,768]{2,1,0:T(8,128)} fusion(f32[2,768,768]{2,1,0:T(8,128)S(1)} %bitcast.92, pred[2]{0:T(512)(128)(4,1)S(1)} %compare_reduce_fusion, f32[2,768,768]{1,2,0:T(8,128)S(1)} %fusion.3, f32[2,768,768]{2,1,0:T(8,128)S(1)} %bitcast.90), kind=kOutput, calls=%fused_computation.3 | convolution fusion | flops 10877534208 | bytes 18874370 | tf_op jit(solution)/shard_map/kil,kml->kim/dot_general | solution.py:187
  739.0 0.6 multiply_subtract_fusion
  (129 shorter events, 3.7 us)
Async XLA Ops:
  7.2 72.1 %all-gather.2.cloned.1.call-start = ((), (), s32[]{:S(2)}) async-start(), calls=%async_computation.1 | async-start | bytes 11796480 | tf_op jit(solution)/shard_map/all_gather | solution.py:92
  11.2 1.3 copy-start.2
  11.2 44.1 %copy-start.17 = (f32[6,768]{1,0:T(8,128)S(1)}, f32[6,768]{1,0:T(8,128)}, u32[]{:S(2)}) copy-start(f32[6,768]{1,0:T(8,128)} %param.13) | copy-start | bytes 55300
  11.2 513.3 %all-reduce.6.cloned.1.call-start = ((), (), s32[]{:S(2)}) async-start(), calls=%async_computation.2 | async-start | bytes 16515072 | tf_op jit(solution)/shard_map/psum | solution.py:173
  12.8 50.4 %copy-start.44 = (s32[7]{0:T(128)S(1)}, s32[7]{0:T(128)}, u32[]{:S(2)}) copy-start(s32[7]{0:T(128)} %param.16) | copy-start | bytes 88
  56.0 3.1 copy-start.28
  57.7 44.6 %copy-start.12 = (bf16[768,768]{1,0:T(8,128)(2,1)}, bf16[768,768]{1,0:T(8,128)(2,1)S(1)}, u32[]{:S(2)}) copy-start(bf16[768,768]{1,0:T(8,128)(2,1)S(1)} %fusion.33) | copy-start | bytes 3538948
  57.7 44.5 %collective-permute-start.1 = (bf16[2,768]{1,0:T(2,128)(2,1)S(1)}, bf16[2,768]{1,0:T(2,128)(2,1)S(1)}, u32[]{:S(2)}, u32[]{:S(2)}) collective-permute-start(bf16[2,768]{1,0:T(2,128)(2,1)S(1)} %get-tuple-element.48), channel_id=1, source_target_pairs={{1,0},{2,1},{3,2},{4,3},{5,4},{6,5},{7,6},{8,7},{9,8},{10,9},{11,1... | collective-permute-start | bytes 9224 | tf_op jit(solution)/shard_map/ppermute | solution.py:31
  59.0 38.4 %collective-permute-start = (bf16[2,768]{1,0:T(2,128)(2,1)S(1)}, bf16[2,768]{1,0:T(2,128)(2,1)S(1)}, u32[]{:S(2)}, u32[]{:S(2)}) collective-permute-start(bf16[2,768]{1,0:T(2,128)(2,1)S(1)} %get-tuple-element.47), channel_id=1, source_target_pairs={{0,1},{1,2},{2,3},{3,4},{4,5},{5,6},{6,7},{7,8},{8,9},{9,10},{10,1... | collective-permute-start | bytes 9224 | tf_op jit(solution)/shard_map/ppermute | solution.py:30
  63.3 24.4 %copy-start.40 = (s32[7]{0:T(128)}, s32[7]{0:T(128)S(1)}, u32[]{:S(2)}) copy-start(s32[7]{0:T(128)S(1)} %compare_select_fusion) | copy-start | bytes 88
  97.5 2.4 copy-start.42
  102.3 2.4 copy-start.35
  102.3 2.4 copy-start.38
  108.3 46.2 %copy-start.9 = (f32[768,768]{1,0:T(8,128)}, f32[768,768]{1,0:T(8,128)S(1)}, u32[]{:S(2)}) copy-start(f32[768,768]{1,0:T(8,128)S(1)} %get-tuple-element.55) | copy-start | bytes 7077892
  149.5 5.0 copy-start.25
  149.5 40.2 %copy-start.23 = (f32[768]{0:T(1024)}, f32[768]{0:T(1024)S(1)}, u32[]{:S(2)}) copy-start(f32[768]{0:T(1024)S(1)} %get-tuple-element.52) | copy-start | bytes 9220
  165.2 2.7 copy-start
  165.2 3.0 copy-start.4
  177.6 3.5 copy-start.1
  181.6 5.6 copy-start.5
  187.1 2.6 copy-start.10
  187.2 2.6 copy-start.26
  187.2 2.6 copy-start.32
  187.2 2.6 copy-start.36
  189.8 6.6 copy-start.6
  189.8 48.7 %copy-start.11 = (f32[768,768]{1,0:T(8,128)S(1)}, f32[768,768]{1,0:T(8,128)}, u32[]{:S(2)}) copy-start(f32[768,768]{1,0:T(8,128)} %copy-done.9) | copy-start | bytes 7077892
  237.9 0.6 copy-start.30
  238.5 3.9 copy-start.13
  238.5 3.9 copy-start.43
  242.4 8.8 %copy-start.14 = (bf16[768,768]{1,0:T(8,128)(2,1)}, bf16[768,768]{1,0:T(8,128)(2,1)S(1)}, u32[]{:S(2)}) copy-start(bf16[768,768]{1,0:T(8,128)(2,1)S(1)} %get-tuple-element.39) | copy-start | bytes 3538948
  246.8 2.2 copy-start.39
  251.2 2.2 copy-start.7
  251.2 2.2 copy-start.24
  251.2 2.2 copy-start.27
  251.2 2.2 copy-start.33
  251.2 2.2 copy-start.37
  253.4 2.8 copy-start.16
  258.4 402.0 %reduce-scatter.2.cloned.1.call-start = ((), (), s32[]{:S(2)}) async-start(), calls=%async_computation.3 | async-start | bytes 11796480 | tf_op jit(solution)/shard_map/reduce_scatter | solution.py:177
  535.1 8.1 %copy-start.41 = (s32[7]{0:T(128)S(1)}, s32[7]{0:T(128)}, u32[]{:S(2)}) copy-start(s32[7]{0:T(128)} %copy-done.40) | copy-start | bytes 88
  581.3 0.7 copy-start.45
  581.3 1.3 copy-start.15
  582.6 3.7 copy-start.22
  582.6 3.7 copy-start.31
  582.6 7.0 copy-start.21
  582.6 7.0 collective-permute-start.2
  586.4 8.6 %collective-permute-start.3 = (bf16[2,768]{1,0:T(2,128)(2,1)S(1)}, bf16[2,768]{1,0:T(2,128)(2,1)S(1)}, u32[]{:S(2)}, u32[]{:S(2)}) collective-permute-start(bf16[2,768]{1,0:T(2,128)(2,1)S(1)} %get-tuple-element.46), channel_id=1, source_target_pairs={{0,1},{1,2},{2,3},{3,4},{4,5},{5,6},{6,7},{7,8},{8,9},{9,10},{10,1... | collective-permute-start | bytes 9224 | tf_op jit(solution)/shard_map/ppermute | solution.py:30
  595.0 2.6 copy-start.3
  595.0 2.6 copy-start.29
  597.6 46.8 %copy-start.34 = (f32[768]{0:T(1024)S(1)}, f32[768]{0:T(1024)}, u32[]{:S(2)}) copy-start(f32[768]{0:T(1024)} %get-tuple-element.49) | copy-start | bytes 9220
  644.4 42.8 %slice-start = ((s8[4718592]{0:T(1024)(128)(4,1)}), s8[524288]{0:T(1024)(128)(4,1)S(1)}, s32[]{:S(2)}) async-start(s8[4718592]{0:T(1024)(128)(4,1)} %bitcast.89), calls=%async_computation.4 | async-start | bytes 1048576
  660.4 12.2 %copy-start.8 = (bf16[2,768,768]{2,1,0:T(8,128)(2,1)S(1)}, bf16[2,768,768]{2,1,0:T(8,128)(2,1)}, u32[]{:S(2)}) copy-start(bf16[2,768,768]{2,1,0:T(8,128)(2,1)} %reduce-scatter.2.cloned.1.call-done) | copy-start | bytes 7077892
  672.6 14.7 %slice-start.1 = ((s8[4718592]{0:T(1024)(128)(4,1)}), s8[4194304]{0:T(1024)(128)(4,1)S(1)}, s32[]{:S(2)}) async-start(s8[4718592]{0:T(1024)(128)(4,1)} %bitcast.89), calls=%async_computation.5 | async-start | bytes 8388608
  687.3 37.6 %slice-start.2 = ((s8[4718592]{0:T(1024)(128)(4,1)}), s8[524288]{0:T(1024)(128)(4,1)S(1)}, s32[]{:S(2)}) async-start(s8[4718592]{0:T(1024)(128)(4,1)} %bitcast.91), calls=%async_computation.6 | async-start | bytes 1048576
  705.2 19.6 %slice-start.3 = ((s8[4718592]{0:T(1024)(128)(4,1)}), s8[4194304]{0:T(1024)(128)(4,1)S(1)}, s32[]{:S(2)}) async-start(s8[4718592]{0:T(1024)(128)(4,1)} %bitcast.91), calls=%async_computation.7 | async-start | bytes 8388608
  724.9 14.1 %copy-start.18 = (f32[6,768]{1,0:T(8,128)S(1)}, f32[6,768]{1,0:T(8,128)}, u32[]{:S(2)}) copy-start(f32[6,768]{1,0:T(8,128)} %param.13) | copy-start | bytes 55300
  724.9 14.1 %copy-start.19 = (f32[6,768]{1,0:T(8,128)S(1)}, f32[6,768]{1,0:T(8,128)}, u32[]{:S(2)}) copy-start(f32[6,768]{1,0:T(8,128)} %param.14) | copy-start | bytes 55300
  724.9 14.1 %copy-start.20 = (f32[6,768]{1,0:T(8,128)S(1)}, f32[6,768]{1,0:T(8,128)}, u32[]{:S(2)}) copy-start(f32[6,768]{1,0:T(8,128)} %param.15) | copy-start | bytes 55300
Sparse Core Ops, SparseCore 0:
  11.3 67.8 all-gather.1
  258.5 266.0 all-reduce.5
  581.4 78.8 reduce-scatter.1
where the time goes:
time: 756 us; the launch traced here: 748 us
  waiting for transfers between devices  295 us (39%)
  blocking collectives  172 us (23%)
  matrix products  130 us (17%)
  local copies, waits for them, and re-layouts  67.7 us (9%)
  other arithmetic  57.3 us (8%)
  between operations  17.5 us (2%)
  starting transfers between devices  9.12 us (1%)
    psum x1, waiting for transfers between devices, per_device(): lax.psum(local_grads.astype(jnp.bfloat16), 'seq').astype(jnp.float32)  266 us
    psum x2, blocking collectives, back_sums(): lax.psum((jnp.sum(grad_normed, axis=0), jnp.sum(grad_normed * normed, axi...  82.7 us
    psum x2, blocking collectives, batch_stats(): lax.psum((jnp.sum(values, axis=0), jnp.sum(values * values, axis=0)), ('s...  82.4 us
    scatter x1, local copies, waits for them, and re-layouts, per_device(): jnp.zeros((slot_total, channels, channels), jnp.float32).at[slot_of_matrix]  28.3 us
    dot_general x1, matrix products, per_device(): jnp.einsum('kij,kjl->kil', left_basis, direction, precision=HIGHEST_PREC)  19.6 us
    dot_general x1, matrix products, per_device(): jnp.einsum('kil,klm->kim', turned, right_basis, precision=HIGHEST_PREC)  17.9 us
    all_gather x1, waiting for transfers between devices, per_device(): lax.all_gather(master.astype(jnp.bfloat16), 'own', axis=0, tiled=True)  16 us
    dot_general x5, matrix products, per_device(): jnp.einsum('ld,cd->lc', grad_padded[4 - offset:4 - offset + positions], w...  15.8 us
  transfers between devices with their start and end apart: 7, of which 3 were waited for; matrix products, arithmetic and copies ran while one was open for 6% of the time, Pallas kernels for 0%

commit v1 on v0

v1 whole, which is shorter than its diff:
```python
import functools
import math

import jax
import jax.numpy as jnp
from jax import lax
from jax.experimental import pallas as pl
from jax.experimental.pallas import tpu as pltpu
from jax.sharding import PartitionSpec as P

NMAT = 7
STEP = 10
NORM_EPS = 1e-05
BETA_ONE = 0.9
BETA_TWO = 0.999
ADAM_EPS = 1e-08
DECAY_RATE = 0.01
LEARN_RATE = 0.02
SMALL_RATE = 0.1
CLIP_RATIO = 0.5
MESH = pl.DeviceIdType.MESH
F32 = jnp.float32
BF16 = jnp.bfloat16

ORDER = (6, 5, 0, 1, 2, 3, 4)
TILE = 256


def mm(a, b):
    return lax.dot_general(a, b, (((1,), (0,)), ((), ())), preferred_element_type=F32)


def mm_t(a, b):
    return lax.dot_general(a, b, (((1,), (1,)), ((), ())), preferred_element_type=F32)


def gelu_both(v):
    k = math.sqrt(2.0 / math.pi)
    sq = v * v
    t = jnp.tanh(v * (k + (k * 0.044715) * sq))
    half = 0.5 + 0.5 * t
    slope = half + (0.5 * v) * (1.0 - t * t) * (k + (3.0 * k * 0.044715) * sq)
    return v * half, slope


def colsum(v):
    return jnp.sum(v, axis=0, keepdims=True)


def kernel(
    dims,
    slot_ref,
    sp_ref,
    dy_ref,
    x_hbm,
    master_hbm,
    pooled_ref,
    ig_ref,
    g_ref,
    gs_ref,
    ssq_ref,
    w,
    mst,
    xf,
    sh,
    d1,
    h,
    a2,
    d2,
    r,
    rd,
    dl,
    dz,
    b,
    a1t,
    rdt,
    snd,
    own,
    rcv,
    fst,
    sec,
    zr,
    zs,
    res,
    stage,
    par,
    ar_val,
    ar_core,
    ar_chip,
    hx_s,
    hx_r,
    hd_s,
    hd_r,
    il,
    sq_all,
    ld_sem,
    w_send,
    w_sib,
    w_x,
    w_y,
    w_z,
    ar_s,
    ar_r,
    ar_s2,
    ar_r2,
    h_s,
    h_r,
    c_s,
    c_r,
    f_s,
    f_r,
    s_s,
    s_r,
    z_s,
    z_r,
    zb_s,
    zb_r,
    g_s,
    g_r,
    q_s,
    q_r,
    g_l,
):
    NX, NY, NZ, cap, rows_total = dims
    pos, ch = dz.shape
    hp = pos // 2
    seq_n, own_n = NZ * NY, NX * 2
    n_dev = seq_n * own_n
    chips = n_dev // 2
    rb = ch // 2 // (NX * NY)
    nt = ch // TILE
    s_ix, o_ix = lax.axis_index("seq"), lax.axis_index("own")
    z, y = s_ix // NY, lax.rem(s_ix, NY)
    x, c = o_ix // 2, lax.rem(o_ix, 2)
    me = s_ix * own_n + o_ix
    inv_n = 1.0 / rows_total

    def dev(z_, y_, x_, c_):
        return (z_ * NY + y_, x_ * 2 + c_)

    def remote(src, dst, ss, rs, to):
        return pltpu.make_async_remote_copy(
            src_ref=src, dst_ref=dst, send_sem=ss, recv_sem=rs, device_id=to, device_id_type=MESH
        )

    def wait_bytes(ref, sem):
        pltpu.make_async_copy(ref, ref, sem).wait()

    sib = dev(z, y, x, 1 - c)

    for j in range(cap):
        pltpu.make_async_copy(master_hbm.at[j], mst.at[j], ld_sem.at[j]).start()
    pltpu.make_async_copy(x_hbm, dz, ld_sem.at[cap]).start()

    barrier = pltpu.get_barrier_semaphore()

    def greet(i, carry):
        p = lax.rem(me + 1 + i, n_dev)
        pl.semaphore_signal(
            barrier, inc=1, device_id=(p // own_n, lax.rem(p, own_n)), device_id_type=MESH
        )
        return carry

    lax.fori_loop(0, n_dev - 1, greet, 0)

    for j in range(cap):
        pltpu.make_async_copy(master_hbm.at[j], mst.at[j], ld_sem.at[j]).wait()
        w[o_ix * cap + j] = mst[j].astype(BF16)
    pl.semaphore_wait(barrier, n_dev - 1)

    thirds = (NX, NY, NZ) == (2, 2, 4)
    QR = 64
    third = ch // 3
    nq = third // QR
    w_base = o_ix * cap
    if thirds:
        is_end = jnp.logical_or(z == 0, z == NZ - 1)
        zp = z + 1 - 2 * lax.rem(z, 2)
        ox = (1 - x) * 2 + c
        to_x, to_y, to_z = dev(z, y, 1 - x, c), dev(z, 1 - y, x, c), dev(zp, y, x, c)
        alpha = jnp.where(is_end, y, 2)
        z_part = jnp.where(is_end, 2, y)

        def piece(slot, part, q):
            return w.at[slot, pl.ds(pl.multiple_of(part * third + q * QR, QR), QR)]

        def each(fn):
            def body(i, carry):
                fn(i, i // nq, lax.rem(i, nq))
                return carry

            lax.fori_loop(0, cap * nq, body, 0)

        def send_x(i, j, q):
            ref = piece(w_base + j, alpha, q)
            remote(ref, ref, w_send.at[0], w_x.at[i], to_x).start()

        each(send_x)
        for j in range(cap):
            ref = w.at[w_base + j]
            remote(ref, ref, w_send.at[0], w_sib.at[0], sib).start()

        def relay(i, j, q):
            rx = piece(ox * cap + j, alpha, q)
            remote(rx, rx, w_send.at[0], w_x.at[i], to_x).wait_recv()
            remote(rx, rx, w_send.at[0], w_z.at[i], to_z).start()

            @pl.when(is_end)
            def _():
                remote(rx, rx, w_send.at[0], w_y.at[i], to_y).start()

            remote(rx, rx, w_send.at[0], w_sib.at[0], sib).start()
            rz = piece(ox * cap + j, z_part, q)
            remote(rz, rz, w_send.at[0], w_z.at[i], to_z).wait_recv()

            @pl.when(jnp.logical_not(is_end))
            def _():
                remote(rz, rz, w_send.at[0], w_y.at[i], to_y).start()

            remote(rz, rz, w_send.at[0], w_sib.at[0], sib).start()

        def last_relay(i, j, q):
            ry = piece(ox * cap + j, 1 - y, q)
            remote(ry, ry, w_send.at[0], w_y.at[i], to_y).wait_recv()
            remote(ry, ry, w_send.at[0], w_sib.at[0], sib).start()

        def weights_first():
            each(relay)

        def weights_end():
            each(last_relay)
            wait_bytes(w.at[pl.ds(0, 2 * cap)], w_sib.at[0])
            wait_bytes(w.at[pl.ds(0, 3 * cap)], w_send.at[0])

    else:

        def send_w(i, carry):
            p = lax.rem(o_ix + 1 + i, own_n)
            ref = w.at[pl.ds(w_base, cap)]
            remote(ref, ref, w_send.at[0], w_sib.at[0], (s_ix, p)).start()
            return carry

        lax.fori_loop(0, own_n - 1, send_w, 0)

        def weights_first():
            pass

        def weights_end():
            wait_bytes(w.at[pl.ds(0, (own_n - 1) * cap)], w_sib.at[0])
            wait_bytes(w.at[pl.ds(0, (own_n - 1) * cap)], w_send.at[0])

    chip = s_ix * NX + x

    def ar_begin(i):
        remote(ar_val.at[i], ar_core.at[i], ar_s.at[i], ar_r.at[i], sib).start()

    def ar_chip_copy(i, k):
        p = lax.rem(chip + 1 + k, chips)
        ref = ar_chip.at[i % ar_chip.shape[0], chip]
        return remote(
            ref, ref, ar_s2.at[i], ar_r2.at[i], (p // NX, lax.rem(p, NX) * 2 + c)
        )

    def ar_mid(i):
        remote(ar_val.at[i], ar_core.at[i], ar_s.at[i], ar_r.at[i], sib).wait()
        ar_chip[i % ar_chip.shape[0], chip] = ar_val[i] + ar_core[i]

        def body(k, carry):
            ar_chip_copy(i, k).start()
            return carry

        lax.fori_loop(0, chips - 1, body, 0)

    def ar_end(i):
        at = i % ar_chip.shape[0]
        wait_bytes(ar_chip.at[at, pl.ds(0, chips - 1)], ar_r2.at[i])
        wait_bytes(ar_chip.at[at, pl.ds(0, chips - 1)], ar_s2.at[i])
        return jnp.sum(ar_chip[at], axis=0)

    pltpu.make_async_copy(x_hbm, dz, ld_sem.at[cap]).wait()
    ts = hp // 3
    total = jnp.zeros((1, ch), F32)
    square = jnp.zeros((1, ch), F32)
    for i in range(3):
        for j in range(ch // 128):
            il[j] = dz[2 * ts * i : 2 * ts * (i + 1), j * 128 : (j + 1) * 128].astype(F32)
        for k in range(2):
            v = jnp.concatenate([il[j, pl.ds(k, ts, stride=2), :] for j in range(ch // 128)], axis=1)
            xf[k * hp + i * ts : k * hp + (i + 1) * ts] = v
            total += colsum(v)
            square += colsum(v * v)
    zero_row = jnp.zeros((1, ch), F32)
    ar_val[0] = jnp.concatenate([total, square, zero_row, zero_row], axis=0)
    ar_begin(0)
    before, after = lax.rem(me + n_dev - 1, n_dev), lax.rem(me + 1, n_dev)
    to_before = (before // own_n, lax.rem(before, own_n))
    to_after = (after // own_n, lax.rem(after, own_n))
    has_before = jnp.where(me > 0, 1.0, 0.0).astype(F32)
    has_after = jnp.where(me < n_dev - 1, 1.0, 0.0).astype(F32)
    hx_s[0] = jnp.concatenate([xf[0:1], xf[hp : hp + 1]], axis=0)
    hx_s[1] = jnp.concatenate([xf[hp - 1 : hp], xf[pos - 1 : pos]], axis=0)
    hx = [
        remote(hx_s.at[0], hx_r.at[1], h_s.at[0], h_r.at[0], to_before),
        remote(hx_s.at[1], hx_r.at[0], h_s.at[1], h_r.at[1], to_after),
    ]
    for cp in hx:
        cp.start()
    ar_mid(0)
    weights_first()
    sums = ar_end(0)
    for cp in hx:
        cp.wait()

    mu1 = sums[0:1] * inv_n
    rstd1 = lax.rsqrt(sums[1:2] * inv_n - mu1 * mu1 + NORM_EPS)
    g1, b1, c1 = sp_ref[0:1], sp_ref[1:2], sp_ref[2:3]
    g2, b2, c2 = sp_ref[3:4], sp_ref[4:5], sp_ref[5:6]
    PAD = 8

    def windows():
        for k in range(2):
            for i in range(3):
                b[k * hp + i * ts : k * hp + (i + 1) * ts] = sh[
                    k, PAD - 1 + i * ts : PAD - 1 + (i + 1) * ts
                ].astype(BF16)
                lo = (4 + k) * hp + i * ts
                b[lo : lo + ts] = sh[k, PAD + 1 + i * ts : PAD + 1 + (i + 1) * ts].astype(BF16)

    for k in range(2):
        for i in range(3):
            lo = k * hp + i * ts
            act, slope = gelu_both((xf[lo : lo + ts] - mu1) * rstd1 * g1 + b1)
            d1[lo : lo + ts] = slope
            b[2 * hp + lo : 2 * hp + lo + ts] = act.astype(BF16)
            sh[k, PAD + i * ts : PAD + (i + 1) * ts] = act
    lead, _ = gelu_both((hx_r[0] - mu1) * rstd1 * g1 + b1)
    trail, _ = gelu_both((hx_r[1] - mu1) * rstd1 * g1 + b1)
    lead, trail = lead * has_before, trail * has_after
    for k in range(2):
        sh[k, PAD - 1 : PAD] = lead[k : k + 1]
        sh[k, PAD + hp : PAD + hp + 1] = trail[k : k + 1]
    windows()
    weights_end()

    slots = [slot_ref[k] for k in range(NMAT)]

    def cols(n):
        return pl.ds(pl.multiple_of(n * TILE, TILE), TILE)

    def over_tiles(fn):
        def body(n, carry):
            fn(cols(n))
            return carry

        lax.fori_loop(0, nt, body, 0)

    def conv_tile(n):
        acc = mm(b[0:pos, :], w[slots[0], :, n])
        for t in range(1, 5):
            acc += mm(b[t * hp : t * hp + pos, :], w[slots[t], :, n])
        acc += sp_ref[2:3, n]
        h[:, n] = acc
        ar_val[1, 0:1, n] = colsum(acc)
        ar_val[1, 1:2, n] = colsum(acc * acc)

    ar_val[1] = jnp.zeros_like(ar_val[1])
    over_tiles(conv_tile)
    ar_begin(1)
    for i in range(nt):
        a1t[i * TILE : (i + 1) * TILE, :] = b[2 * hp : 4 * hp, i * TILE : (i + 1) * TILE].T
    ar_mid(1)
    sums = ar_end(1)
    mu2 = sums[0:1] * inv_n
    rstd2 = lax.rsqrt(sums[1:2] * inv_n - mu2 * mu2 + NORM_EPS)
    for k in range(2):
        for i in range(3):
            lo = k * hp + i * ts
            act, slope = gelu_both((h[lo : lo + ts] - mu2) * rstd2 * g2 + b2)
            d2[lo : lo + ts] = slope
            a2[lo : lo + ts] = act.astype(BF16)

    ar_val[2] = jnp.zeros_like(ar_val[2])
    par[...] = jnp.concatenate([mu2, rstd2, zero_row, zero_row], axis=0)

    def mix_tile(n):
        v = h[:, n] + mm(a2[...], w[slots[5], :, n]) + sp_ref[5:6, n]
        r[:, n] = v
        rd[:, n] = (v[:hp] - v[hp:]).astype(BF16)

    over_tiles(mix_tile)

    def pool_tile(n):
        diff = mm(rd[...], w[slots[6], :, n])
        t = 0.5 * jnp.tanh(0.5 * diff)
        p0, p1 = 0.5 + t, 0.5 - t
        r0, r1 = r[0:hp, n], r[hp:pos, n]
        dy = dy_ref[:, n].astype(F32)
        pooled_ref[:, n] = (p0 * r0 + p1 * r1).astype(BF16)
        dl[:, n] = (p0 * p1 * dy * (r0 - r1)).astype(BF16)
        mst[0, 0:hp, n] = p0 * dy
        mst[0, hp:pos, n] = p1 * dy

    over_tiles(pool_tile)

    def resid_tile(n):
        v = mm_t(dl[...], w[slots[6], n, :])
        v0 = mst[0, 0:hp, n] + v
        v1 = mst[0, hp:pos, n] - v
        mst[0, 0:hp, n] = v0
        mst[0, hp:pos, n] = v1
        dz[0:hp, n] = v0.astype(BF16)
        dz[hp:pos, n] = v1.astype(BF16)
        ar_val[2, 2:3, n] = colsum(v0) + colsum(v1)

    over_tiles(resid_tile)

    def branch_tile(n):
        v = mm_t(dz[...], w[slots[5], n, :]) * d2[:, n]
        mst[1, :, n] = v
        xhat = (h[:, n] - par[0:1, n]) * par[1:2, n]
        ar_val[2, 0:1, n] = colsum(v)
        ar_val[2, 1:2, n] = colsum(v * xhat)

    over_tiles(branch_tile)
    ar_begin(2)
    hd_s[0] = jnp.concatenate(
        [v for ref in (mst.at[0], mst.at[1], h) for v in (ref[0:1], ref[hp : hp + 1])]
        + [zero_row, zero_row],
        axis=0,
    )
    hd_s[1] = jnp.concatenate(
        [v for ref in (mst.at[0], mst.at[1], h) for v in (ref[hp - 1 : hp], ref[pos - 1 : pos])]
        + [zero_row, zero_row],
        axis=0,
    )
    hd = [
        remote(hd_s.at[0], hd_r.at[1], h_s.at[2], h_r.at[2], to_before),
        remote(hd_s.at[1], hd_r.at[0], h_s.at[3], h_r.at[3], to_after),
    ]
    for cp in hd:
        cp.start()

    half = ch // 2

    def put_gradient(p, lhs, rhs):
        for dst, core in ((snd, 1 - c), (own, c)):
            left = lhs(pl.ds(pl.multiple_of(core * half, half), half))

            def tile(n, dst=dst, left=left):
                v = mm(left(), rhs(n)).astype(BF16)
                for i in range(NX * NY):
                    dst[p, i // NY, i % NY, :, n] = v[i * rb : (i + 1) * rb]

            over_tiles(tile)
            if dst is snd:
                core_copy(p).start()

    def core_copy(p):
        return remote(snd.at[p], rcv.at[p], c_s.at[p], c_r.at[p], sib)

    def x_first(p):
        return p % 2 == 0

    def first_copy(p, k):
        if x_first(p):
            to = lax.rem(x + 1 + k, NX)
            return remote(
                own.at[p, to], fst.at[p, NX - 2 - k], f_s.at[p, k], f_r.at[p, NX - 2 - k], dev(z, y, to, c)
            )
        to = lax.rem(y + 1 + k, NY)
        return remote(
            own.at[p, :, to], fst.at[p, NY - 2 - k], f_s.at[p, k], f_r.at[p, NY - 2 - k], dev(z, to, x, c)
        )

    def second_copy(p, k):
        if x_first(p):
            to = lax.rem(y + 1 + k, NY)
            return remote(
                own.at[p, x, to], sec.at[p, NY - 2 - k], s_s.at[p, k], s_r.at[p, NY - 2 - k], dev(z, to, x, c)
            )
        to = lax.rem(x + 1 + k, NX)
        return remote(
            own.at[p, to, y], sec.at[p, NX - 2 - k], s_s.at[p, k], s_r.at[p, NX - 2 - k], dev(z, y, to, c)
        )

    def wait_all(copy, p, n):
        for k in range(n - 1):
            copy(p, k).wait_send()
        for k in range(n - 1):
            copy(p, k).wait_recv()

    def step_first(p):
        core_copy(p).wait()
        for i in range(NX):
            for j in range(NY):
                own[p, i, j] = (own[p, i, j].astype(F32) + rcv[p, i, j].astype(F32)).astype(BF16)
        for k in range((NX if x_first(p) else NY) - 1):
            first_copy(p, k).start()

    def step_second(p):
        n, m = (NX, NY) if x_first(p) else (NY, NX)
        wait_all(first_copy, p, n)
        for j in range(m):
            at = (p, x, j) if x_first(p) else (p, j, y)
            v = own[at].astype(F32)
            for k in range(n - 1):
                v += fst[p, k, j].astype(F32)
            own[at] = v.astype(BF16)
        for k in range(m - 1):
            second_copy(p, k).start()

    root = (NZ - 1) // 2
    up, down = dev(lax.rem(z + 1, NZ), y, x, c), dev(lax.rem(z + NZ - 1, NZ), y, x, c)

    def z_copy(p, side):
        return remote(
            zs.at[p], zr.at[p, side], z_s.at[p], z_r.at[p, side], up if side == 0 else down
        )

    def bc_copy(p, side):
        return remote(
            res.at[p], res.at[p], zb_s.at[p, side], zb_r.at[p], down if side == 0 else up
        )

    def step_sum(p):
        m = NY if x_first(p) else NX
        wait_all(second_copy, p, m)
        v = own[p, x, y].astype(F32)
        for k in range(m - 1):
            v += sec[p, k].astype(F32)
        zs[p] = v.astype(BF16)
        if root > 0:

            @pl.when(z == 0)
            def _():
                z_copy(p, 0).start()

        if root < NZ - 1:

            @pl.when(z == NZ - 1)
            def _():
                z_copy(p, 1).start()

    def step_pass(p):
        for side, inner in ((0, jnp.logical_and(z > 0, z < root)), (1, jnp.logical_and(z > root, z < NZ - 1))):

            @pl.when(inner)
            def _(side=side):
                z_copy(p, side).wait_recv()
                zs[p] = (zs[p].astype(F32) + zr[p, side].astype(F32)).astype(BF16)
                z_copy(p, side).start()

    def step_root(p):
        @pl.when(z == root)
        def _():
            v = zs[p].astype(F32)
            if root > 0:
                z_copy(p, 0).wait_recv()
                v += zr[p, 0].astype(F32)
            if root < NZ - 1:
                z_copy(p, 1).wait_recv()
                v += zr[p, 1].astype(F32)
            res[p] = v.astype(BF16)
            if root > 0:
                bc_copy(p, 0).start()
            if root < NZ - 1:
                bc_copy(p, 1).start()

    def step_spread(p):
        @pl.when(z != root)
        def _():
            bc_copy(p, 0).wait_recv()

        for side, inner in ((0, jnp.logical_and(z > 0, z < root)), (1, jnp.logical_and(z > root, z < NZ - 1))):

            @pl.when(inner)
            def _(side=side):
                bc_copy(p, side).start()

    def step_done(p):
        @pl.when(z != root)
        def _():
            z_copy(p, 0).wait_send()

        for side, sent in ((0, jnp.logical_and(z > 0, z <= root)), (1, jnp.logical_and(z >= root, z < NZ - 1))):

            @pl.when(sent)
            def _(side=side):
                bc_copy(p, side).wait_send()

    for i in range(nt):
        rdt[i * TILE : (i + 1) * TILE, :] = rd[:, i * TILE : (i + 1) * TILE].T
    ar_mid(2)
    put_gradient(0, lambda rows: lambda: rdt[rows, :], lambda n: dl[:, n])
    for i in range(nt):
        b[i * TILE : (i + 1) * TILE, :] = a2[:, i * TILE : (i + 1) * TILE].T
    sums = ar_end(2)
    s2, q2, e2 = sums[0:1], sums[1:2], sums[2:3]
    put_gradient(1, lambda rows: lambda: b[rows, :], lambda n: dz[:, n])
    step_first(0)

    scale2 = rstd2 * g2

    def dh_of(dr, dn, hid):
        xhat = (hid - mu2) * rstd2
        return dr + scale2 * (dn - s2 * inv_n - xhat * (q2 * inv_n))

    e1_local = jnp.zeros((1, ch), F32)
    for k in range(2):
        for i in range(3):
            lo = k * hp + i * ts
            v = dh_of(mst[0, lo : lo + ts], mst[1, lo : lo + ts], h[lo : lo + ts])
            e1_local += colsum(v)
            sh[k, PAD + i * ts : PAD + (i + 1) * ts] = v
            b[2 * hp + lo : 2 * hp + lo + ts] = v.astype(BF16)
    for cp in hd:
        cp.wait()
    lead = dh_of(hd_r[0, 0:2], hd_r[0, 2:4], hd_r[0, 4:6]) * has_before
    trail = dh_of(hd_r[1, 0:2], hd_r[1, 2:4], hd_r[1, 4:6]) * has_after
    for k in range(2):
        sh[k, PAD - 1 : PAD] = lead[k : k + 1]
        sh[k, PAD + hp : PAD + hp + 1] = trail[k : k + 1]
    windows()
    step_first(1)

    def tap(t):
        lo = (4 - t) * hp
        put_gradient(2 + t, lambda rows: lambda: a1t[rows, :], lambda n: b[lo : lo + pos, n])

    tap(0)
    step_second(0)
    tap(1)
    step_first(2)
    step_second(1)
    tap(2)
    step_first(3)
    step_sum(0)
    tap(3)
    step_first(4)
    step_sum(1)
    step_pass(0)
    tap(4)
    step_first(5)
    step_second(2)
    step_root(0)
    step_pass(1)

    ar_val[3] = jnp.zeros_like(ar_val[3])
    ar_val[3, 2:3] = e1_local
    par[...] = jnp.concatenate([mu1, rstd1, zero_row, zero_row], axis=0)

    def input_tile(n):
        acc = mm_t(b[4 * hp : 4 * hp + pos, :], w[slots[0], n, :])
        for t in range(1, 5):
            lo = (4 - t) * hp
            acc += mm_t(b[lo : lo + pos, :], w[slots[t], n, :])
        v = acc * d1[:, n]
        mst[1, :, n] = v
        xhat = (xf[:, n] - par[0:1, n]) * par[1:2, n]
        ar_val[3, 0:1, n] = colsum(v)
        ar_val[3, 1:2, n] = colsum(v * xhat)

    over_tiles(input_tile)
    ar_begin(3)
    step_first(6)
    step_second(3)
    ar_mid(3)
    step_spread(0)
    step_root(1)
    step_sum(2)
    step_second(4)
    sums = ar_end(3)
    s1, q1, e1 = sums[0:1], sums[1:2], sums[2:3]
    gs_ref[...] = jnp.concatenate([q1, s1, e1, q2, s2, e2], axis=0)
    scale1 = rstd1 * g1
    for i in range(3):
        for k in range(2):
            lo = k * hp + i * ts
            xhat = (xf[lo : lo + ts] - mu1) * rstd1
            v = scale1 * (mst[1, lo : lo + ts] - s1 * inv_n - xhat * (q1 * inv_n))
            for j in range(ch // 128):
                il[j, pl.ds(k, ts, stride=2), :] = v[:, j * 128 : (j + 1) * 128]
        for j in range(ch // 128):
            ig_ref[2 * i * ts : 2 * (i + 1) * ts, j * 128 : (j + 1) * 128] = il[j].astype(BF16)

    step_pass(2)
    step_sum(3)
    step_second(5)
    step_spread(1)
    step_root(2)
    step_pass(3)
    step_sum(4)
    step_second(6)
    step_spread(2)
    step_root(3)
    step_pass(4)
    step_sum(5)
    step_spread(3)
    step_root(4)
    step_pass(5)
    step_sum(6)
    step_spread(4)
    step_root(5)
    step_pass(6)
    step_root(6)
    step_spread(5)
    step_spread(6)

    plane = NX * NY * 2
    mine = (x * NY + y) * 2 + c
    for s in range(own_n * cap):
        at = jnp.int32(0)
        for p in range(NMAT):
            at = jnp.maximum(at, jnp.where(slots[ORDER[p]] == s, p, 0))
        stage[s] = res[at]

    def plane_of(k):
        p = lax.rem(mine + 1 + k, plane)
        return p, p // (2 * NY), lax.rem(p // 2, NY), lax.rem(p, 2)

    def gather_send(k):
        _, px, py, pc = plane_of(k)
        src = stage.at[pl.ds((px * 2 + pc) * cap, cap)]
        return remote(src, g_ref.at[:, c, x, y], g_s.at[k], g_r.at[plane - 2 - k], dev(z, py, px, pc))

    def gather_recv(k):
        _, px, py, pc = plane_of(k)
        src = stage.at[pl.ds((px * 2 + pc) * cap, cap)]
        return remote(src, g_ref.at[:, pc, px, py], g_s.at[k], g_r.at[k], dev(z, py, px, pc))

    def square_copy(k):
        _, px, py, pc = plane_of(k)
        ref = sq_all.at[mine]
        return remote(ref, ref, q_s.at[0], q_r.at[0], dev(z, py, px, pc))

    for k in range(plane - 1):
        gather_send(k).start()
    keep = pltpu.make_async_copy(
        stage.at[pl.ds(o_ix * cap, cap)], g_ref.at[:, c, x, y], g_l.at[0]
    )
    keep.start()
    sq = jnp.zeros((8, ch), F32)
    for p in range(NMAT):
        v = res[p].astype(F32)
        v = v * v
        for i in range(rb // 8):
            sq += v[i * 8 : (i + 1) * 8]
    sq_all[mine] = sq
    for k in range(plane - 1):
        square_copy(k).start()
    for p in range(NMAT):
        step_done(p)
    wait_bytes(sq_all.at[pl.ds(0, plane - 1)], q_r.at[0])
    wait_bytes(sq_all.at[pl.ds(0, plane - 1)], q_s.at[0])
    ssq_ref[...] = jnp.sum(sq_all[...], axis=0)
    for k in range(plane - 1):
        gather_send(k).wait_send()
    for k in range(plane - 1):
        gather_recv(k).wait_recv()
    keep.wait()


def adam_moments(grads, first_old, second_old):
    first_new = BETA_ONE * first_old + (1.0 - BETA_ONE) * grads
    second_new = BETA_TWO * second_old + (1.0 - BETA_TWO) * grads * grads
    direction = (
        first_new
        / (1.0 - BETA_ONE**STEP)
        / (jnp.sqrt(second_new / (1.0 - BETA_TWO**STEP)) + ADAM_EPS)
    )
    return (first_new, second_new, direction)


def per_device(
    inputs,
    cotangent,
    small_params,
    small_first,
    small_second,
    slot_of_matrix,
    master,
    first_moment,
    second_moment,
    left_basis,
    right_basis,
):
    pos, ch = inputs.shape
    seq_n, own_n = lax.axis_size("seq"), lax.axis_size("own")
    nx = own_n // 2
    ny = nx
    nz = seq_n // ny
    cap = master.shape[0]
    hp = pos // 2
    slots = cap * own_n
    chips = seq_n * nx
    rb = ch // 2 // (nx * ny)
    plane = nx * ny * 2
    nn = max(nx, ny)
    dma = pltpu.SemaphoreType.DMA
    vm = pltpu.VMEM
    scratch = [
        vm((slots, ch, ch), BF16),
        vm((max(cap, 2), ch, ch), F32),
        vm((pos, ch), F32),
        vm((2, hp + 16, ch), F32),
        vm((pos, ch), F32),
        vm((pos, ch), F32),
        vm((pos, ch), BF16),
        vm((pos, ch), F32),
        vm((pos, ch), F32),
        vm((hp, ch), BF16),
        vm((hp, ch), BF16),
        vm((pos, ch), BF16),
        vm((6 * hp, ch), BF16),
        vm((ch, pos), BF16),
        vm((ch, hp), BF16),
        vm((NMAT, nx, ny, rb, ch), BF16),
        vm((NMAT, nx, ny, rb, ch), BF16),
        vm((NMAT, nx, ny, rb, ch), BF16),
        vm((NMAT, nn - 1, nn, rb, ch), BF16),
        vm((NMAT, nn - 1, rb, ch), BF16),
        vm((NMAT, 2, rb, ch), BF16),
        vm((NMAT, rb, ch), BF16),
        vm((NMAT, rb, ch), BF16),
        vm((slots, rb, ch), BF16),
        vm((4, ch), F32),
        vm((4, 4, ch), F32),
        vm((4, 4, ch), F32),
        vm((4 if chips <= 16 else 2, chips, 4, ch), F32),
        vm((2, 2, ch), F32),
        vm((2, 2, ch), F32),
        vm((2, 8, ch), F32),
        vm((2, 8, ch), F32),
        vm((ch // 128, hp // 3 * 2, 128), F32),
        vm((plane, 8, ch), F32),
        dma((cap + 1,)),
        dma((1,)),
        dma((1,)),
        dma((cap * 4,)),
        dma((cap * 4,)),
        dma((cap * 4,)),
        dma((4,)),
        dma((4,)),
        dma((4,)),
        dma((4,)),
        dma((4,)),
        dma((4,)),
        dma((NMAT,)),
        dma((NMAT,)),
        dma((NMAT, nn - 1)),
        dma((NMAT, nn - 1)),
        dma((NMAT, nn - 1)),
        dma((NMAT, nn - 1)),
        dma((NMAT,)),
        dma((NMAT, 2)),
        dma((NMAT, 2)),
        dma((NMAT,)),
        dma((plane - 1,)),
        dma((plane - 1,)),
        dma((1,)),
        dma((1,)),
        dma((1,)),
    ]
    in_vmem = pl.BlockSpec(memory_space=pltpu.VMEM)
    anywhere = pl.BlockSpec(memory_space=pl.ANY)
    pooled, input_grad, owned, small_grad, squares = pl.pallas_call(
        functools.partial(kernel, (nx, ny, nz, cap, pos * seq_n * own_n)),
        out_shape=(
            jax.ShapeDtypeStruct((hp, ch), BF16),
            jax.ShapeDtypeStruct((pos, ch), BF16),
            jax.ShapeDtypeStruct((cap, 2, nx, ny, rb, ch), BF16),
            jax.ShapeDtypeStruct((6, ch), F32),
            jax.ShapeDtypeStruct((8, ch), F32),
        ),
        in_specs=[pl.BlockSpec(memory_space=pltpu.SMEM), in_vmem, in_vmem, anywhere, anywhere],
        out_specs=(in_vmem, in_vmem, anywhere, in_vmem, in_vmem),
        scratch_shapes=scratch,
        compiler_params=pltpu.CompilerParams(
            collective_id=0, has_side_effects=True, vmem_limit_bytes=63 * 2**20
        ),
    )(slot_of_matrix, small_params, cotangent, inputs, master)
    owned = owned.reshape(cap, ch, ch)
    grad_norm = jnp.sqrt(jnp.sum(squares) + jnp.sum(small_grad * small_grad))
    factor = jnp.minimum(1.0, CLIP_RATIO * ch * math.sqrt(NMAT) / (grad_norm + 1e-06))
    turned = jnp.einsum(
        "kji,kjl->kil", left_basis.astype(BF16), owned, preferred_element_type=F32
    )
    turned = factor * jnp.einsum(
        "kil,klm->kim", turned.astype(BF16), right_basis.astype(BF16), preferred_element_type=F32
    )
    first_new, second_new, direction = adam_moments(turned, first_moment, second_moment)
    back_turn = jnp.einsum(
        "kij,kjl->kil", left_basis.astype(BF16), direction.astype(BF16), preferred_element_type=F32
    )
    back_turn = jnp.einsum(
        "kil,kml->kim", back_turn.astype(BF16), right_basis.astype(BF16), preferred_element_type=F32
    )
    master_new = master - LEARN_RATE * (back_turn + DECAY_RATE * master)
    slot_ids = lax.axis_index("own") * cap + jnp.arange(cap, dtype=jnp.int32)
    is_used = jnp.any(slot_ids[:, None] == slot_of_matrix[None, :], axis=1)[:, None, None]
    new_master = jnp.where(is_used, master_new, master)
    new_first = jnp.where(is_used, first_new, first_moment)
    new_second = jnp.where(is_used, second_new, second_moment)
    small_first_new, small_second_new, small_dir = adam_moments(
        small_grad * factor, small_first, small_second
    )
    new_small = small_params - SMALL_RATE * (small_dir + DECAY_RATE * small_params)
    return (
        pooled,
        input_grad,
        grad_norm,
        new_master,
        new_first,
        new_second,
        new_small,
        small_first_new,
        small_second_new,
    )


def solution(mesh):
    rows, owned, same = P(("seq", "own"), None), P("own", None, None), P()
    return jax.shard_map(
        per_device,
        mesh=mesh,
        in_specs=(rows, rows, same, same, same, same, owned, owned, owned, owned, owned),
        out_specs=(rows, rows, same, owned, owned, owned, same, same, same),
        check_vma=False,
    )
```

time: 756 us -> 228 us (0.30); the launches traced: 748 us -> 227 us
  waiting for transfers between devices: 295 us -> 0 us
  Pallas kernels: 0 us -> 188 us
  blocking collectives: 172 us -> 0 us
  matrix products: 130 us -> 31.1 us
  local copies, waits for them, and re-layouts: 67.7 us -> 1.86 us
  other arithmetic: 57.3 us -> 3.53 us
  between operations: 17.5 us -> 3.25 us
  starting transfers between devices: 9.12 us -> 0 us
    psum x1 -> x0, waiting for transfers between devices: 266 us -> none  [per_device(): lax.psum(local_grads.astype(jnp.bfloat16), 'seq').astype(jnp.float32)]
    pallas_call x0 -> x1, Pallas kernels: none -> 188 us  [per_device(): pl.pallas_call(functools.partial(kernel, (nx, ny, nz, cap, pos * seq_n *...]
    psum x5 -> x0, blocking collectives: 172 us -> none  [the longest x2 82.7 us: back_sums(): lax.psum((jnp.sum(grad_normed, axis=0), jnp.sum(grad_normed * normed, axi...]
    dot_general x25 -> x2, matrix products: 130 us -> 31.1 us  [the longest x1 17.8 us: per_device(): jnp.einsum('kil,kml->kim', back_turn.astype(BF16), right_basis.astype(BF1...]
    convert_element_type x7 -> x0, other arithmetic: 30.5 us -> none  [the longest x1 10.5 us: per_device(): lax.psum(local_grads.astype(jnp.bfloat16), 'seq').astype(jnp.float32)]
    scatter x1 -> x0, local copies, waits for them, and re-layouts: 28.3 us -> none  [per_device(): jnp.zeros((slot_total, channels, channels), jnp.float32).at[slot_of_matrix]]
    all_gather x1 -> x0, waiting for transfers between devices: 16 us -> none  [per_device(): lax.all_gather(master.astype(jnp.bfloat16), 'own', axis=0, tiled=True)]
    reduce_scatter x1 -> x0, waiting for transfers between devices: 12.6 us -> none  [per_device(): lax.psum_scatter(placed.astype(jnp.bfloat16), 'own', scatter_dimension=0,...]
  transfers between devices with their start and end apart: 7 -> 0, of which waited for: 3 -> 0; matrix products, arithmetic and copies ran while one was open for 6% -> 0% of each run, Pallas kernels for 0% -> 0%
where the time goes in v1:
time: 228 us; the launch traced here: 227 us
  Pallas kernels  188 us (82%)
  matrix products  31.1 us (14%)
  other arithmetic  3.53 us (2%)
  between operations  3.25 us (1%)
    pallas_call x1, Pallas kernels, per_device(): pl.pallas_call(functools.partial(kernel, (nx, ny, nz, cap, pos * seq_n *...  188 us
    dot_general x1, matrix products, per_device(): jnp.einsum('kil,kml->kim', back_turn.astype(BF16), right_basis.astype(BF1...  17.8 us
    dot_general x1, matrix products, per_device(): jnp.einsum('kil,klm->kim', turned.astype(BF16), right_basis.astype(BF16),...  13.3 us

profile of v1, /device:TPU:0, one launch (start us, length us, event | category | flops | bytes accessed | tf_op | source)
XLA Modules:
  0.0 227.4 jit_solution(13219624008304763098)
XLA Ops:
  0.6 0.0 copy-start.6
  0.7 187.7 %shard_map.178 = (bf16[384,768]{1,0:T(8,128)(2,1)}, bf16[768,768]{1,0:T(8,128)(2,1)}, bf16[2,2,2,2,96,768]{5,4,3,2,1,0:T(8,128)(2,1)}, f32[6,768]{1,0:T(8,128)}, f32[8,768]{1,0:T(8,128)}) custom-call(s32[7]{0:T(128)} %slot_ref.1, f32[6,768]{1,0:T(8,128)} %sp_ref.1, bf16[384,768]{1,0:T(8,128)(2,1)} %dy_ref.1, bf16[768,768]{1,0:T(8,128)(2,1)} %x_hbm.1, ...), custom_call_target="tpu_custom_call" | custom-call | tf_op jit(solution)/shard_map/pallas_call | solution.py:866
  188.3 1.3 reduce_sum.18
  189.7 1.3 multiply_reduce_fusion
  192.4 0.0 copy-done.6
  192.4 0.2 compare_reduce_fusion
  192.6 13.3 %fusion.2 = (f32[2,768,768]{2,1,0:T(8,128)}, f32[2,768,768]{2,1,0:T(8,128)}, f32[2,768,768]{2,1,0:T(8,128)}) fusion(f32[2,768,768]{2,1,0:T(8,128)} %param.19, f32[]{:T(128)S(6)} %min_shard_map.3, pred[2]{0:T(512)(128)(4,1)S(1)} %compare_reduce_fusion, f32[2,768,768]{2,1,0:T(8,128)} %param.18, f32[2,768,768]{2,1,0:T(8,128)} %param.21, ...), kind=kOutput, calls=%fused_computation.6 | convolution fusion | flops 3639214080 | bytes 35389448 | tf_op jit(solution)/shard_map/kil,klm->kim/dot_general | solution.py:888
  205.9 0.0 copy-start.2
  205.9 0.0 copy-start.3
  205.9 0.0 copy-start.4
  205.9 0.0 copy-start.5
  206.0 0.0 copy-start.1
  206.0 0.0 copy-start
  206.0 17.8 %subtract_select_fusion = f32[2,768,768]{2,1,0:T(8,128)} fusion(f32[2,768,768]{2,1,0:T(8,128)} %master_hbm.1, pred[2]{0:T(512)(128)(4,1)S(1)} %compare_reduce_fusion, f32[2,768,768]{2,1,0:T(8,128)} %get-tuple-element.24, f32[2,768,768]{2,1,0:T(8,128)} %param.18, f32[2,768,768]{2,1,0:T(8,128)} %param.19, f32[]{:T(128)S(6)} %min_shard_map.3, ...), kind=kOutput, calls=%fused_computation | convolution fusion | flops 3648651264 | bytes 33030150 | tf_op jit(solution)/shard_map/kil,kml->kim/dot_general | solution.py:895
  223.8 0.0 copy-done.2
  223.8 0.0 copy-done.3
  223.8 0.0 copy-done.4
  223.8 0.0 copy-done.5
  223.8 0.6 multiply_subtract_fusion
  224.5 0.0 copy-done.1
  224.5 0.8 copy.22
  225.3 0.0 copy-done
  225.3 1.0 copy.23
  (1 shorter events, 0.0 us)
Async XLA Ops:
  0.6 191.7 %copy-start.6 = (s32[7]{0:T(128)S(1)}, s32[7]{0:T(128)}, u32[]{:S(2)}) copy-start(s32[7]{0:T(128)} %slot_ref.1) | copy-start | bytes 88
  205.9 17.9 %copy-start.2 = (f32[6,768]{1,0:T(8,128)S(1)}, f32[6,768]{1,0:T(8,128)}, u32[]{:S(2)}) copy-start(f32[6,768]{1,0:T(8,128)} %sp_ref.1) | copy-start | bytes 55300
  205.9 17.9 %copy-start.3 = (f32[6,768]{1,0:T(8,128)S(1)}, f32[6,768]{1,0:T(8,128)}, u32[]{:S(2)}) copy-start(f32[6,768]{1,0:T(8,128)} %get-tuple-element.17) | copy-start | bytes 55300
  205.9 17.9 %copy-start.4 = (f32[6,768]{1,0:T(8,128)S(1)}, f32[6,768]{1,0:T(8,128)}, u32[]{:S(2)}) copy-start(f32[6,768]{1,0:T(8,128)} %param.14) | copy-start | bytes 55300
  205.9 17.9 %copy-start.5 = (f32[6,768]{1,0:T(8,128)S(1)}, f32[6,768]{1,0:T(8,128)}, u32[]{:S(2)}) copy-start(f32[6,768]{1,0:T(8,128)} %param.15) | copy-start | bytes 55300
  206.0 18.5 %copy-start.1 = (bf16[384,768]{1,0:T(8,128)(2,1)S(1)}, bf16[384,768]{1,0:T(8,128)(2,1)}, u32[]{:S(2)}) copy-start(bf16[384,768]{1,0:T(8,128)(2,1)} %get-tuple-element.34) | copy-start | bytes 1769476
  206.0 19.3 %copy-start = (bf16[768,768]{1,0:T(8,128)(2,1)S(1)}, bf16[768,768]{1,0:T(8,128)(2,1)}, u32[]{:S(2)}) copy-start(bf16[768,768]{1,0:T(8,128)(2,1)} %get-tuple-element.35) | copy-start | bytes 3538948

commit v2 on v1

--- a/solution.py
+++ b/solution.py
@@ -96,6 +96,7 @@
     ld_sem,
     w_send,
     w_sib,
+    w_xs,
     w_x,
     w_y,
     w_z,
@@ -184,53 +185,60 @@
         def piece(slot, part, q):
             return w.at[slot, pl.ds(pl.multiple_of(part * third + q * QR, QR), QR)]
 
-        def each(fn):
-            def body(i, carry):
-                fn(i, i // nq, lax.rem(i, nq))
-                return carry
-
-            lax.fori_loop(0, cap * nq, body, 0)
-
-        def send_x(i, j, q):
-            ref = piece(w_base + j, alpha, q)
-            remote(ref, ref, w_send.at[0], w_x.at[i], to_x).start()
-
-        each(send_x)
+        WINDOW = 2
+
+        def x_copy(i):
+            ref = piece(w_base + i // nq, alpha, i % nq)
+            return remote(ref, ref, w_xs.at[i], w_x.at[i], to_x)
+
+        for i in range(WINDOW):
+            x_copy(i).start()
         for j in range(cap):
             ref = w.at[w_base + j]
             remote(ref, ref, w_send.at[0], w_sib.at[0], sib).start()
 
-        def relay(i, j, q):
-            rx = piece(ox * cap + j, alpha, q)
-            remote(rx, rx, w_send.at[0], w_x.at[i], to_x).wait_recv()
-            remote(rx, rx, w_send.at[0], w_z.at[i], to_z).start()
-
-            @pl.when(is_end)
-            def _():
-                remote(rx, rx, w_send.at[0], w_y.at[i], to_y).start()
-
-            remote(rx, rx, w_send.at[0], w_sib.at[0], sib).start()
-            rz = piece(ox * cap + j, z_part, q)
-            remote(rz, rz, w_send.at[0], w_z.at[i], to_z).wait_recv()
-
-            @pl.when(jnp.logical_not(is_end))
-            def _():
-                remote(rz, rz, w_send.at[0], w_y.at[i], to_y).start()
-
-            remote(rz, rz, w_send.at[0], w_sib.at[0], sib).start()
-
-        def last_relay(i, j, q):
-            ry = piece(ox * cap + j, 1 - y, q)
-            remote(ry, ry, w_send.at[0], w_y.at[i], to_y).wait_recv()
-            remote(ry, ry, w_send.at[0], w_sib.at[0], sib).start()
-
-        def weights_first():
-            each(relay)
+        n_pieces = cap * nq
+        LAG_Z, LAG_Y = 2, 4
+        n_steps = n_pieces + LAG_Y
+
+        def pass_on(ref, sem, to):
+            remote(ref, ref, w_send.at[0], sem, to).start()
+
+        def weights_step(i):
+            if i < n_pieces:
+                ref = piece(ox * cap + i // nq, alpha, i % nq)
+                remote(ref, ref, w_xs.at[i], w_x.at[i], to_x).wait_recv()
+                x_copy(i).wait_send()
+                if i + WINDOW < n_pieces:
+                    x_copy(i + WINDOW).start()
+                pass_on(ref, w_z.at[i], to_z)
+
+                @pl.when(is_end)
+                def _():
+                    pass_on(ref, w_y.at[i], to_y)
+
+                pass_on(ref, w_sib.at[0], sib)
+            k = i - LAG_Z
+            if 0 <= k < n_pieces:
+                ref_z = piece(ox * cap + k // nq, z_part, k % nq)
+                remote(ref_z, ref_z, w_send.at[0], w_z.at[k], to_z).wait_recv()
+
+                @pl.when(jnp.logical_not(is_end))
+                def _():
+                    pass_on(ref_z, w_y.at[k], to_y)
+
+                pass_on(ref_z, w_sib.at[0], sib)
+            k = i - LAG_Y
+            if 0 <= k < n_pieces:
+                ref_y = piece(ox * cap + k // nq, 1 - y, k % nq)
+                remote(ref_y, ref_y, w_send.at[0], w_y.at[k], to_y).wait_recv()
+                pass_on(ref_y, w_sib.at[0], sib)
 
         def weights_end():
-            each(last_relay)
             wait_bytes(w.at[pl.ds(0, 2 * cap)], w_sib.at[0])
-            wait_bytes(w.at[pl.ds(0, 3 * cap)], w_send.at[0])
+            wait_bytes(w.at[pl.ds(0, 2 * cap)], w_send.at[0])
+            wait_bytes(w.at[0, pl.ds(0, 2 * third)], w_send.at[0])
+            wait_bytes(w.at[0, pl.ds(0, 2 * third)], w_send.at[0])
 
     else:
 
@@ -242,7 +250,9 @@
 
         lax.fori_loop(0, own_n - 1, send_w, 0)
 
-        def weights_first():
+        n_steps = 0
+
+        def weights_step(i):
             pass
 
         def weights_end():
@@ -306,7 +316,8 @@
     for cp in hx:
         cp.start()
     ar_mid(0)
-    weights_first()
+    for i in range(min(2, n_steps)):
+        weights_step(i)
     sums = ar_end(0)
     for cp in hx:
         cp.wait()
@@ -333,6 +344,8 @@
             d1[lo : lo + ts] = slope
             b[2 * hp + lo : 2 * hp + lo + ts] = act.astype(BF16)
             sh[k, PAD + i * ts : PAD + (i + 1) * ts] = act
+            if 2 + 3 * k + i < n_steps:
+                weights_step(2 + 3 * k + i)
     lead, _ = gelu_both((hx_r[0] - mu1) * rstd1 * g1 + b1)
     trail, _ = gelu_both((hx_r[1] - mu1) * rstd1 * g1 + b1)
     lead, trail = lead * has_before, trail * has_after
@@ -340,6 +353,8 @@
         sh[k, PAD - 1 : PAD] = lead[k : k + 1]
         sh[k, PAD + hp : PAD + hp + 1] = trail[k : k + 1]
     windows()
+    for i in range(8, n_steps):
+        weights_step(i)
     weights_end()
 
     slots = [slot_ref[k] for k in range(NMAT)]
@@ -379,6 +394,192 @@
             d2[lo : lo + ts] = slope
             a2[lo : lo + ts] = act.astype(BF16)
 
+    half = ch // 2
+    halves = own.shape[1]
+    rh = rb // halves
+
+    def put_gradient(p, lhs, rhs):
+        def tile(n):
+            v = mm(lhs[...], rhs(n))
+            keep = jnp.where(c == 0, v[:half], v[half:]).astype(BF16)
+            give = jnp.where(c == 0, v[half:], v[:half]).astype(BF16)
+            for i in range(NX * NY):
+                for k in range(halves):
+                    at = (i * halves + k) * rh
+                    own[p, k, i // NY, i % NY, :, n] = keep[at : at + rh]
+                    snd[p, k, i // NY, i % NY, :, n] = give[at : at + rh]
+
+        over_tiles(tile)
+        core_copy(p).start()
+
+    def core_copy(p):
+        return remote(snd.at[p], rcv.at[p], c_s.at[p], c_r.at[p], sib)
+
+    def first_copies(p):
+        made = []
+        for k in range(NX - 1):
+            to = lax.rem(x + 1 + k, NX)
+            at = NX - 2 - k
+            made.append(remote(own.at[p, 0, to], fst.at[p, 0, at], f_s.at[p, 0, k], f_r.at[p, 0, at], dev(z, y, to, c)))
+        for k in range(NY - 1 if halves > 1 else 0):
+            to = lax.rem(y + 1 + k, NY)
+            at = NY - 2 - k
+            made.append(remote(own.at[p, 1, :, to], fst.at[p, 1, at], f_s.at[p, 1, k], f_r.at[p, 1, at], dev(z, to, x, c)))
+        return made
+
+    def second_copies(p):
+        made = []
+        for k in range(NY - 1):
+            to = lax.rem(y + 1 + k, NY)
+            at = NY - 2 - k
+            made.append(remote(own.at[p, 0, x, to], sec.at[p, 0, at], s_s.at[p, 0, k], s_r.at[p, 0, at], dev(z, to, x, c)))
+        for k in range(NX - 1 if halves > 1 else 0):
+            to = lax.rem(x + 1 + k, NX)
+            at = NX - 2 - k
+            made.append(remote(own.at[p, 1, to, y], sec.at[p, 1, at], s_s.at[p, 1, k], s_r.at[p, 1, at], dev(z, y, to, c)))
+        return made
+
+    def wait_all(copies):
+        for cp in copies:
+            cp.wait_send()
+        for cp in copies:
+            cp.wait_recv()
+
+    def step_first(p):
+        core_copy(p).wait()
+        for k in range(halves):
+            for i in range(NX):
+                for j in range(NY):
+                    own[p, k, i, j] = (own[p, k, i, j].astype(F32) + rcv[p, k, i, j].astype(F32)).astype(BF16)
+        for cp in first_copies(p):
+            cp.start()
+
+    def step_second(p):
+        wait_all(first_copies(p))
+        for k in range(halves):
+            n, m = (NX, NY) if k == 0 else (NY, NX)
+            for j in range(m):
+                at = (p, 0, x, j) if k == 0 else (p, 1, j, y)
+                v = own[at].astype(F32)
+                for i in range(n - 1):
+                    v += fst[p, k, i, j].astype(F32)
+                own[at] = v.astype(BF16)
+        for cp in second_copies(p):
+            cp.start()
+
+    chain = NZ == 4 and halves == 2
+    is_outer = jnp.logical_or(z == 0, z == NZ - 1)
+    is_inner = jnp.logical_not(is_outer)
+    inner = jnp.where(z < 2, 1, 2)
+    my_half = jnp.clip(z - 1, 0, 1)
+
+    def end_copy(p):
+        return remote(zs.at[p], zr.at[p, 0], z_s.at[p, 0], z_r.at[p, 0], dev(inner, y, x, c))
+
+    def swap_copy(p, k):
+        return remote(zs.at[p, k], zr.at[p, 1, k], z_s.at[p, 1], z_r.at[p, 1], dev(lax.rem(3 - z + NZ, NZ), y, x, c))
+
+    def spread_copy(p, k, i):
+        return remote(res.at[p, k], res.at[p, k], zb_s.at[p, i], zb_r.at[p, k], dev(lax.rem(z + 1 + i, NZ), y, x, c))
+
+    def gather_copy(p, at):
+        return remote(zs.at[p], zr.at[p, at], z_s.at[p, 0], z_r.at[p, at], dev(0, y, x, c))
+
+    def whole_copy(p, i):
+        return remote(res.at[p], res.at[p], zb_s.at[p, i], zb_r.at[p, 0], dev(lax.rem(z + 1 + i, NZ), y, x, c))
+
+    def step_sum(p):
+        wait_all(second_copies(p))
+        for k in range(halves):
+            v = own[p, k, x, y].astype(F32)
+            for i in range((NY if k == 0 else NX) - 1):
+                v += sec[p, k, i].astype(F32)
+            zs[p, k] = v.astype(BF16)
+        if chain:
+
+            @pl.when(is_outer)
+            def _():
+                end_copy(p).start()
+
+        else:
+
+            @pl.when(z > 0)
+            def _():
+                gather_copy(p, z - 1).start()
+
+    def step_pass(p):
+        if chain:
+
+            @pl.when(is_inner)
+            def _():
+                end_copy(p).wait_recv()
+                zs[p] = (zs[p].astype(F32) + zr[p, 0].astype(F32)).astype(BF16)
+                swap_copy(p, 1 - my_half).start()
+
+    def step_root(p):
+        if chain:
+
+            @pl.when(is_inner)
+            def _():
+                swap_copy(p, my_half).wait_recv()
+                res[p, my_half] = (zs[p, my_half].astype(F32) + zr[p, 1, my_half].astype(F32)).astype(BF16)
+                for i in range(NZ - 1):
+                    spread_copy(p, my_half, i).start()
+
+        else:
+
+            @pl.when(z == 0)
+            def _():
+                v = zs[p].astype(F32)
+                for i in range(NZ - 1):
+                    gather_copy(p, i).wait_recv()
+                    v += zr[p, i].astype(F32)
+                res[p] = v.astype(BF16)
+                for i in range(NZ - 1):
+                    whole_copy(p, i).start()
+
+    def step_spread(p):
+        if chain:
+
+            @pl.when(is_outer)
+            def _():
+                for k in range(2):
+                    spread_copy(p, k, 0).wait_recv()
+
+            @pl.when(is_inner)
+            def _():
+                spread_copy(p, 1 - my_half, 0).wait_recv()
+
+        else:
+
+            @pl.when(z > 0)
+            def _():
+                whole_copy(p, 0).wait_recv()
+
+    def step_done(p):
+        if chain:
+
+            @pl.when(is_outer)
+            def _():
+                end_copy(p).wait_send()
+
+            @pl.when(is_inner)
+            def _():
+                swap_copy(p, 1 - my_half).wait_send()
+                for i in range(NZ - 1):
+                    spread_copy(p, my_half, i).wait_send()
+
+        else:
+
+            @pl.when(z > 0)
+            def _():
+                gather_copy(p, z - 1).wait_send()
+
+            @pl.when(z == 0)
+            def _():
+                for i in range(NZ - 1):
+                    whole_copy(p, i).wait_send()
+
     ar_val[2] = jnp.zeros_like(ar_val[2])
     par[...] = jnp.concatenate([mu2, rstd2, zero_row, zero_row], axis=0)
 
@@ -388,6 +589,8 @@
         rd[:, n] = (v[:hp] - v[hp:]).astype(BF16)
 
     over_tiles(mix_tile)
+    for i in range(nt):
+        rdt[i * TILE : (i + 1) * TILE, :] = rd[:, i * TILE : (i + 1) * TILE].T
 
     def pool_tile(n):
         diff = mm(rd[...], w[slots[6], :, n])
@@ -401,6 +604,7 @@
         mst[0, hp:pos, n] = p1 * dy
 
     over_tiles(pool_tile)
+    put_gradient(0, rdt, lambda n: dl[:, n])
 
     def resid_tile(n):
         v = mm_t(dl[...], w[slots[6], n, :])
@@ -413,6 +617,7 @@
         ar_val[2, 2:3, n] = colsum(v0) + colsum(v1)
 
     over_tiles(resid_tile)
+    step_first(0)
 
     def branch_tile(n):
         v = mm_t(dz[...], w[slots[5], n, :]) * d2[:, n]
@@ -440,164 +645,14 @@
     for cp in hd:
         cp.start()
 
-    half = ch // 2
-
-    def put_gradient(p, lhs, rhs):
-        for dst, core in ((snd, 1 - c), (own, c)):
-            left = lhs(pl.ds(pl.multiple_of(core * half, half), half))
-
-            def tile(n, dst=dst, left=left):
-                v = mm(left(), rhs(n)).astype(BF16)
-                for i in range(NX * NY):
-                    dst[p, i // NY, i % NY, :, n] = v[i * rb : (i + 1) * rb]
-
-            over_tiles(tile)
-            if dst is snd:
-                core_copy(p).start()
-
-    def core_copy(p):
-        return remote(snd.at[p], rcv.at[p], c_s.at[p], c_r.at[p], sib)
-
-    def x_first(p):
-        return p % 2 == 0
-
-    def first_copy(p, k):
-        if x_first(p):
-            to = lax.rem(x + 1 + k, NX)
-            return remote(
-                own.at[p, to], fst.at[p, NX - 2 - k], f_s.at[p, k], f_r.at[p, NX - 2 - k], dev(z, y, to, c)
-            )
-        to = lax.rem(y + 1 + k, NY)
-        return remote(
-            own.at[p, :, to], fst.at[p, NY - 2 - k], f_s.at[p, k], f_r.at[p, NY - 2 - k], dev(z, to, x, c)
-        )
-
-    def second_copy(p, k):
-        if x_first(p):
-            to = lax.rem(y + 1 + k, NY)
-            return remote(
-                own.at[p, x, to], sec.at[p, NY - 2 - k], s_s.at[p, k], s_r.at[p, NY - 2 - k], dev(z, to, x, c)
-            )
-        to = lax.rem(x + 1 + k, NX)
-        return remote(
-            own.at[p, to, y], sec.at[p, NX - 2 - k], s_s.at[p, k], s_r.at[p, NX - 2 - k], dev(z, y, to, c)
-        )
-
-    def wait_all(copy, p, n):
-        for k in range(n - 1):
-            copy(p, k).wait_send()
-        for k in range(n - 1):
-            copy(p, k).wait_recv()
-
-    def step_first(p):
-        core_copy(p).wait()
-        for i in range(NX):
-            for j in range(NY):
-                own[p, i, j] = (own[p, i, j].astype(F32) + rcv[p, i, j].astype(F32)).astype(BF16)
-        for k in range((NX if x_first(p) else NY) - 1):
-            first_copy(p, k).start()
-
-    def step_second(p):
-        n, m = (NX, NY) if x_first(p) else (NY, NX)
-        wait_all(first_copy, p, n)
-        for j in range(m):
-            at = (p, x, j) if x_first(p) else (p, j, y)
-            v = own[at].astype(F32)
-            for k in range(n - 1):
-                v += fst[p, k, j].astype(F32)
-            own[at] = v.astype(BF16)
-        for k in range(m - 1):
-            second_copy(p, k).start()
-
-    root = (NZ - 1) // 2
-    up, down = dev(lax.rem(z + 1, NZ), y, x, c), dev(lax.rem(z + NZ - 1, NZ), y, x, c)
-
-    def z_copy(p, side):
-        return remote(
-            zs.at[p], zr.at[p, side], z_s.at[p], z_r.at[p, side], up if side == 0 else down
-        )
-
-    def bc_copy(p, side):
-        return remote(
-            res.at[p], res.at[p], zb_s.at[p, side], zb_r.at[p], down if side == 0 else up
-        )
-
-    def step_sum(p):
-        m = NY if x_first(p) else NX
-        wait_all(second_copy, p, m)
-        v = own[p, x, y].astype(F32)
-        for k in range(m - 1):
-            v += sec[p, k].astype(F32)
-        zs[p] = v.astype(BF16)
-        if root > 0:
-
-            @pl.when(z == 0)
-            def _():
-                z_copy(p, 0).start()
-
-        if root < NZ - 1:
-
-            @pl.when(z == NZ - 1)
-            def _():
-                z_copy(p, 1).start()
-
-    def step_pass(p):
-        for side, inner in ((0, jnp.logical_and(z > 0, z < root)), (1, jnp.logical_and(z > root, z < NZ - 1))):
-
-            @pl.when(inner)
-            def _(side=side):
-                z_copy(p, side).wait_recv()
-                zs[p] = (zs[p].astype(F32) + zr[p, side].astype(F32)).astype(BF16)
-                z_copy(p, side).start()
-
-    def step_root(p):
-        @pl.when(z == root)
-        def _():
-            v = zs[p].astype(F32)
-            if root > 0:
-                z_copy(p, 0).wait_recv()
-                v += zr[p, 0].astype(F32)
-            if root < NZ - 1:
-                z_copy(p, 1).wait_recv()
-                v += zr[p, 1].astype(F32)
-            res[p] = v.astype(BF16)
-            if root > 0:
-                bc_copy(p, 0).start()
-            if root < NZ - 1:
-                bc_copy(p, 1).start()
-
-    def step_spread(p):
-        @pl.when(z != root)
-        def _():
-            bc_copy(p, 0).wait_recv()
-
-        for side, inner in ((0, jnp.logical_and(z > 0, z < root)), (1, jnp.logical_and(z > root, z < NZ - 1))):
-
-            @pl.when(inner)
-            def _(side=side):
-                bc_copy(p, side).start()
-
-    def step_done(p):
-        @pl.when(z != root)
-        def _():
-            z_copy(p, 0).wait_send()
-
-        for side, sent in ((0, jnp.logical_and(z > 0, z <= root)), (1, jnp.logical_and(z >= root, z < NZ - 1))):
-
-            @pl.when(sent)
-            def _(side=side):
-                bc_copy(p, side).wait_send()
-
-    for i in range(nt):
-        rdt[i * TILE : (i + 1) * TILE, :] = rd[:, i * TILE : (i + 1) * TILE].T
-    ar_mid(2)
-    put_gradient(0, lambda rows: lambda: rdt[rows, :], lambda n: dl[:, n])
     for i in range(nt):
         b[i * TILE : (i + 1) * TILE, :] = a2[:, i * TILE : (i + 1) * TILE].T
+    ar_mid(2)
+    put_gradient(1, b.at[pl.ds(0, ch)], lambda n: dz[:, n])
+    step_second(0)
     sums = ar_end(2)
     s2, q2, e2 = sums[0:1], sums[1:2], sums[2:3]
-    put_gradient(1, lambda rows: lambda: b[rows, :], lambda n: dz[:, n])
-    step_first(0)
+    step_first(1)
 
     scale2 = rstd2 * g2
 
@@ -621,29 +676,24 @@
         sh[k, PAD - 1 : PAD] = lead[k : k + 1]
         sh[k, PAD + hp : PAD + hp + 1] = trail[k : k + 1]
     windows()
-    step_first(1)
 
     def tap(t):
         lo = (4 - t) * hp
-        put_gradient(2 + t, lambda rows: lambda: a1t[rows, :], lambda n: b[lo : lo + pos, n])
+        put_gradient(2 + t, a1t, lambda n: b[lo : lo + pos, n])
 
     tap(0)
-    step_second(0)
+    step_second(1)
     tap(1)
     step_first(2)
-    step_second(1)
+    step_sum(0)
     tap(2)
     step_first(3)
-    step_sum(0)
     tap(3)
+    tap(4)
+    step_pass(0)
+    step_sum(1)
+    step_second(2)
     step_first(4)
-    step_sum(1)
-    step_pass(0)
-    tap(4)
-    step_first(5)
-    step_second(2)
-    step_root(0)
-    step_pass(1)
 
     ar_val[3] = jnp.zeros_like(ar_val[3])
     ar_val[3, 2:3] = e1_local
@@ -660,15 +710,24 @@
         ar_val[3, 0:1, n] = colsum(v)
         ar_val[3, 1:2, n] = colsum(v * xhat)
 
-    over_tiles(input_tile)
+    input_tile(cols(0))
+    step_second(3)
+    step_first(5)
+    step_root(0)
+    step_pass(1)
+    for i in range(1, nt - 1):
+        input_tile(cols(i))
+    step_second(4)
+    step_first(6)
+    step_sum(2)
+    input_tile(cols(nt - 1))
     ar_begin(3)
-    step_first(6)
-    step_second(3)
+    step_root(1)
+    step_spread(0)
     ar_mid(3)
-    step_spread(0)
-    step_root(1)
-    step_sum(2)
-    step_second(4)
+    step_second(5)
+    step_sum(3)
+    step_pass(2)
     sums = ar_end(3)
     s1, q1, e1 = sums[0:1], sums[1:2], sums[2:3]
     gs_ref[...] = jnp.concatenate([q1, s1, e1, q2, s2, e2], axis=0)
@@ -683,25 +742,22 @@
         for j in range(ch // 128):
             ig_ref[2 * i * ts : 2 * (i + 1) * ts, j * 128 : (j + 1) * 128] = il[j].astype(BF16)
 
-    step_pass(2)
-    step_sum(3)
-    step_second(5)
+    step_second(6)
+    step_sum(4)
+    step_pass(3)
+    step_root(2)
     step_spread(1)
-    step_root(2)
-    step_pass(3)
-    step_sum(4)
-    step_second(6)
+    step_sum(5)
+    step_pass(4)
+    step_root(3)
     step_spread(2)
-    step_root(3)
-    step_pass(4)
-    step_sum(5)
+    step_sum(6)
+    step_pass(5)
+    step_root(4)
     step_spread(3)
-    step_root(4)
-    step_pass(5)
-    step_sum(6)
+    step_pass(6)
+    step_root(5)
     step_spread(4)
-    step_root(5)
-    step_pass(6)
     step_root(6)
     step_spread(5)
     step_spread(6)
@@ -741,10 +797,11 @@
     keep.start()
     sq = jnp.zeros((8, ch), F32)
     for p in range(NMAT):
-        v = res[p].astype(F32)
-        v = v * v
-        for i in range(rb // 8):
-            sq += v[i * 8 : (i + 1) * 8]
+        for k in range(halves):
+            v = res[p, k].astype(F32)
+            v = v * v
+            for i in range(rh // 8):
+                sq += v[i * 8 : (i + 1) * 8]
     sq_all[mine] = sq
     for k in range(plane - 1):
         square_copy(k).start()
@@ -760,30 +817,153 @@
     keep.wait()
 
 
-def adam_moments(grads, first_old, second_old):
+def adam(grads, first_old, second_old):
     first_new = BETA_ONE * first_old + (1.0 - BETA_ONE) * grads
     second_new = BETA_TWO * second_old + (1.0 - BETA_TWO) * grads * grads
-    direction = (
-        first_new
-        / (1.0 - BETA_ONE**STEP)
-        / (jnp.sqrt(second_new / (1.0 - BETA_TWO**STEP)) + ADAM_EPS)
+    direction = (first_new * (1.0 / (1.0 - BETA_ONE**STEP))) / (
+        jnp.sqrt(second_new * (1.0 / (1.0 - BETA_TWO**STEP))) + ADAM_EPS
     )
-    return (first_new, second_new, direction)
-
-
-def per_device(
-    inputs,
-    cotangent,
-    small_params,
-    small_first,
-    small_second,
-    slot_of_matrix,
+    return first_new, second_new, direction
+
+
+def optimizer_kernel(
+    used_ref,
+    ssq_ref,
+    gs_ref,
+    sp_ref,
+    sf_ref,
+    ss_ref,
+    g_hbm,
+    left_hbm,
+    right_hbm,
+    first_hbm,
+    second_hbm,
+    master_hbm,
+    norm_ref,
+    nsp_ref,
+    nsf_ref,
+    nss_ref,
+    nmaster_hbm,
+    nfirst_hbm,
+    nsecond_hbm,
+    g,
+    left,
+    right,
+    first,
+    second,
     master,
-    first_moment,
-    second_moment,
-    left_basis,
-    right_basis,
+    left_low,
+    left_t,
+    right_low,
+    mid,
+    turn,
+    in_sem,
+    out_sem,
 ):
+    cap, ch, _ = g.shape
+    nt = ch // TILE
+    sources = (g_hbm, right_hbm, left_hbm, first_hbm, second_hbm, master_hbm)
+    places = (g, right, left, first, second, master)
+
+    def load(i, j):
+        return pltpu.make_async_copy(sources[i].at[j], places[i].at[j], in_sem.at[i, j])
+
+    def save(i, j):
+        src = (first, second, master)[i]
+        dst = (nfirst_hbm, nsecond_hbm, nmaster_hbm)[i]
+        return pltpu.make_async_copy(src.at[j], dst.at[j], out_sem.at[i, j])
+
+    for j in range(cap):
+        for i in range(6):
+            load(i, j).start()
+
+    gs = gs_ref[...]
+    norm = jnp.sqrt(
+        jnp.sum(jnp.sum(ssq_ref[...], axis=0, keepdims=True), axis=1, keepdims=True)
+        + jnp.sum(jnp.sum(gs * gs, axis=0, keepdims=True), axis=1, keepdims=True)
+    )
+    norm_ref[...] = norm
+    factor = jnp.minimum(1.0, CLIP_RATIO * ch * math.sqrt(NMAT) / (norm + 1e-06))
+    small_first, small_second, small_dir = adam(gs * factor, sf_ref[...], ss_ref[...])
+    nsf_ref[...] = small_first
+    nss_ref[...] = small_second
+    nsp_ref[...] = sp_ref[...] - SMALL_RATE * (small_dir + DECAY_RATE * sp_ref[...])
+
+    def over_tiles(fn):
+        def body(n, carry):
+            fn(pl.ds(pl.multiple_of(n * TILE, TILE), TILE))
+            return carry
+
+        lax.fori_loop(0, nt, body, 0)
+
+    for j in range(cap):
+        used = used_ref[j] > 0
+        load(0, j).wait()
+        load(1, j).wait()
+        right_low[...] = right[j].astype(BF16)
+
+        def mid_tile(n):
+            mid[:, n] = mm(g[j], right_low[:, n]).astype(BF16)
+
+        over_tiles(mid_tile)
+        load(2, j).wait()
+        left_low[...] = left[j].astype(BF16)
+        for i in range(nt):
+            left_t[i * TILE : (i + 1) * TILE, :] = left_low[:, i * TILE : (i + 1) * TILE].T
+        load(3, j).wait()
+        load(4, j).wait()
+
+        def moment_tile(n):
+            grads = factor * mm(left_t[...], mid[:, n])
+            f_old, s_old = first[j, :, n], second[j, :, n]
+            f_new, s_new, direction = adam(grads, f_old, s_old)
+            first[j, :, n] = jnp.where(used, f_new, f_old)
+            second[j, :, n] = jnp.where(used, s_new, s_old)
+            turn[:, n] = direction.astype(BF16)
+
+        over_tiles(moment_tile)
+        save(0, j).start()
+        save(1, j).start()
+
+        def back_tile(n):
+            mid[:, n] = mm(left_low[...], turn[:, n]).astype(BF16)
+
+        over_tiles(back_tile)
+        load(5, j).wait()
+
+        def master_tile(n):
+            old = master[j, :, n]
+            step = mm_t(mid[...], right_low[n, :]) + DECAY_RATE * old
+            master[j, :, n] = jnp.where(used, old - LEARN_RATE * step, old)
+
+        over_tiles(master_tile)
+        save(2, j).start()
+    for j in range(cap):
+        for i in range(3):
+            save(i, j).wait()
+
+
+def optimizer(used, squares, small_grad, small_params, small_first, small_second, owned, left, right, first, second, master):
+    cap, ch, _ = master.shape
+    vm, dma = pltpu.VMEM, pltpu.SemaphoreType.DMA
+    in_vmem = pl.BlockSpec(memory_space=pltpu.VMEM)
+    anywhere = pl.BlockSpec(memory_space=pl.ANY)
+    big = jax.ShapeDtypeStruct((cap, ch, ch), F32)
+    small = jax.ShapeDtypeStruct((6, ch), F32)
+    return pl.pallas_call(
+        optimizer_kernel,
+        out_shape=(jax.ShapeDtypeStruct((1, 1), F32), small, small, small, big, big, big),
+        in_specs=[pl.BlockSpec(memory_space=pltpu.SMEM)] + [in_vmem] * 5 + [anywhere] * 6,
+        out_specs=(in_vmem,) * 4 + (anywhere,) * 3,
+        scratch_shapes=[vm((cap, ch, ch), BF16)]
+        + [vm((cap, ch, ch), F32)] * 5
+        + [vm((ch, ch), BF16)] * 5
+        + [dma((6, cap)), dma((3, cap))],
+        compiler_params=pltpu.CompilerParams(vmem_limit_bytes=60 * 2**20),
+    )(used, squares, small_grad, small_params, small_first, small_second, owned, left, right, first, second, master)
+
+
+def block_and_grads(inputs, cotangent, small_params, slot_of_matrix, master):
     pos, ch = inputs.shape
     seq_n, own_n = lax.axis_size("seq"), lax.axis_size("own")
     nx = own_n // 2
@@ -796,6 +976,8 @@
     rb = ch // 2 // (nx * ny)
     plane = nx * ny * 2
     nn = max(nx, ny)
+    halves = 2 if rb % 32 == 0 else 1
+    rh = rb // halves
     dma = pltpu.SemaphoreType.DMA
     vm = pltpu.VMEM
     scratch = [
@@ -814,15 +996,15 @@
         vm((6 * hp, ch), BF16),
         vm((ch, pos), BF16),
         vm((ch, hp), BF16),
-        vm((NMAT, nx, ny, rb, ch), BF16),
-        vm((NMAT, nx, ny, rb, ch), BF16),
-        vm((NMAT, nx, ny, rb, ch), BF16),
-        vm((NMAT, nn - 1, nn, rb, ch), BF16),
-        vm((NMAT, nn - 1, rb, ch), BF16),
-        vm((NMAT, 2, rb, ch), BF16),
-        vm((NMAT, rb, ch), BF16),
-        vm((NMAT, rb, ch), BF16),
-        vm((slots, rb, ch), BF16),
+        vm((NMAT, halves, nx, ny, rh, ch), BF16),
+        vm((NMAT, halves, nx, ny, rh, ch), BF16),
+        vm((NMAT, halves, nx, ny, rh, ch), BF16),
+        vm((NMAT, halves, nn - 1, nn, rh, ch), BF16),
+        vm((NMAT, halves, nn - 1, rh, ch), BF16),
+        vm((NMAT, 2 if nz == 4 else nz - 1, halves, rh, ch), BF16),
+        vm((NMAT, halves, rh, ch), BF16),
+        vm((NMAT, halves, rh, ch), BF16),
+        vm((slots, halves, rh, ch), BF16),
         vm((4, ch), F32),
         vm((4, 4, ch), F32),
         vm((4, 4, ch), F32),
@@ -839,6 +1021,7 @@
         dma((cap * 4,)),
         dma((cap * 4,)),
         dma((cap * 4,)),
+        dma((cap * 4,)),
         dma((4,)),
         dma((4,)),
         dma((4,)),
@@ -847,14 +1030,14 @@
         dma((4,)),
         dma((NMAT,)),
         dma((NMAT,)),
-        dma((NMAT, nn - 1)),
-        dma((NMAT, nn - 1)),
-        dma((NMAT, nn - 1)),
-        dma((NMAT, nn - 1)),
-        dma((NMAT,)),
+        dma((NMAT, halves, nn - 1)),
+        dma((NMAT, halves, nn - 1)),
+        dma((NMAT, halves, nn - 1)),
+        dma((NMAT, halves, nn - 1)),
         dma((NMAT, 2)),
+        dma((NMAT, max(2, nz - 1))),
+        dma((NMAT, nz - 1)),
         dma((NMAT, 2)),
-        dma((NMAT,)),
         dma((plane - 1,)),
         dma((plane - 1,)),
         dma((1,)),
@@ -863,12 +1046,12 @@
     ]
     in_vmem = pl.BlockSpec(memory_space=pltpu.VMEM)
     anywhere = pl.BlockSpec(memory_space=pl.ANY)
-    pooled, input_grad, owned, small_grad, squares = pl.pallas_call(
+    return pl.pallas_call(
         functools.partial(kernel, (nx, ny, nz, cap, pos * seq_n * own_n)),
         out_shape=(
             jax.ShapeDtypeStruct((hp, ch), BF16),
             jax.ShapeDtypeStruct((pos, ch), BF16),
-            jax.ShapeDtypeStruct((cap, 2, nx, ny, rb, ch), BF16),
+            jax.ShapeDtypeStruct((cap, 2, nx, ny, halves, rh, ch), BF16),
             jax.ShapeDtypeStruct((6, ch), F32),
             jax.ShapeDtypeStruct((8, ch), F32),
         ),
@@ -879,36 +1062,46 @@
             collective_id=0, has_side_effects=True, vmem_limit_bytes=63 * 2**20
         ),
     )(slot_of_matrix, small_params, cotangent, inputs, master)
-    owned = owned.reshape(cap, ch, ch)
-    grad_norm = jnp.sqrt(jnp.sum(squares) + jnp.sum(small_grad * small_grad))
-    factor = jnp.minimum(1.0, CLIP_RATIO * ch * math.sqrt(NMAT) / (grad_norm + 1e-06))
-    turned = jnp.einsum(
-        "kji,kjl->kil", left_basis.astype(BF16), owned, preferred_element_type=F32
+
+
+def per_device(
+    inputs,
+    cotangent,
+    small_params,
+    small_first,
+    small_second,
+    slot_of_matrix,
+    master,
+    first_moment,
+    second_moment,
+    left_basis,
+    right_basis,
+):
+    cap, ch = master.shape[0], master.shape[2]
+    own_n = lax.axis_size("own")
+    pooled, input_grad, owned, small_grad, squares = block_and_grads(
+        inputs, cotangent, small_params, slot_of_matrix, master
     )
-    turned = factor * jnp.einsum(
-        "kil,klm->kim", turned.astype(BF16), right_basis.astype(BF16), preferred_element_type=F32
+    slot_ids = lax.axis_index("own") * cap + jnp.arange(cap, dtype=jnp.int32)
+    used = jnp.any(slot_ids[:, None] == slot_of_matrix[None, :], axis=1).astype(jnp.int32)
+    grad_norm, new_small, small_first_new, small_second_new, new_master, new_first, new_second = optimizer(
+        used,
+        squares,
+        small_grad,
+        small_params,
+        small_first,
+        small_second,
+        owned.reshape(cap, ch, ch),
+        left_basis,
+        right_basis,
+        first_moment,
+        second_moment,
+        master,
     )
-    first_new, second_new, direction = adam_moments(turned, first_moment, second_moment)
-    back_turn = jnp.einsum(
-        "kij,kjl->kil", left_basis.astype(BF16), direction.astype(BF16), preferred_element_type=F32
-    )
-    back_turn = jnp.einsum(
-        "kil,kml->kim", back_turn.astype(BF16), right_basis.astype(BF16), preferred_element_type=F32
-    )
-    master_new = master - LEARN_RATE * (back_turn + DECAY_RATE * master)
-    slot_ids = lax.axis_index("own") * cap + jnp.arange(cap, dtype=jnp.int32)
-    is_used = jnp.any(slot_ids[:, None] == slot_of_matrix[None, :], axis=1)[:, None, None]
-    new_master = jnp.where(is_used, master_new, master)
-    new_first = jnp.where(is_used, first_new, first_moment)
-    new_second = jnp.where(is_used, second_new, second_moment)
-    small_first_new, small_second_new, small_dir = adam_moments(
-        small_grad * factor, small_first, small_second
-    )
-    new_small = small_params - SMALL_RATE * (small_dir + DECAY_RATE * small_params)
     return (
         pooled,
         input_grad,
-        grad_norm,
+        grad_norm.reshape(()),
         new_master,
         new_first,
         new_second,

time: 228 us -> 178 us (0.78)
  matrix products: 31.1 us -> 0 us
  Pallas kernels: 188 us -> 174 us
  between operations: 3.25 us -> 0.69 us
    dot_general x2 -> x0, matrix products: 31.1 us -> none  [the longest x1 17.8 us: per_device(): jnp.einsum('kil,kml->kim', back_turn.astype(BF16), right_basis.astype(BF1...]
    pallas_call x1 -> x2, Pallas kernels: 188 us -> 174 us  [the longest x1 153 us: block_and_grads(): pl.pallas_call(functools.partial(kernel, (nx, ny, nz, cap, pos * seq_n *...]
    reduce_sum x2 -> x0, other arithmetic: 2.7 us -> none  [per_device(): grad_norm = jnp.sqrt(jnp.sum(squares) + jnp.sum(small_grad * small_grad))]
where the time goes in v2:
time: 178 us
  Pallas kernels  174 us (98%)
  local copies, waits for them, and re-layouts  1.84 us (1%)
    pallas_call x1, Pallas kernels, block_and_grads(): pl.pallas_call(functools.partial(kernel, (nx, ny, nz, cap, pos * seq_n *...  153 us
    pallas_call x1, Pallas kernels, optimizer(): pl.pallas_call(optimizer_kernel, out_shape=(jax.ShapeDtypeStruct((1, 1),...  20.8 us

profile of v2, /device:TPU:0, one launch (start us, length us, event | category | flops | bytes accessed | tf_op | source)
XLA Modules:
  0.0 177.9 jit_solution(15572011858682755691)
XLA Ops:
  0.7 0.8 compare_reduce_fusion
  1.5 0.5 convert_element_type.3.used_ref
  2.0 153.2 %shard_map.178 = (bf16[384,768]{1,0:T(8,128)(2,1)}, bf16[768,768]{1,0:T(8,128)(2,1)}, bf16[2,2,2,2,2,48,768]{6,5,4,3,2,1,0:T(8,128)(2,1)}, f32[6,768]{1,0:T(8,128)}, f32[8,768]{1,0:T(8,128)}) custom-call(s32[7]{0:T(128)} %slot_ref.1, f32[6,768]{1,0:T(8,128)} %sp_ref.3, bf16[384,768]{1,0:T(8,128)(2,1)} %dy_ref.1, bf16[768,768]{1,0:T(8,128)(2,1)} %x_hbm.1, ...), custom_call_target="tpu_custom_call" | custom-call | tf_op jit(solution)/shard_map/pallas_call | solution.py:1049
  155.2 0.0 copy-start.1
  155.3 0.0 copy-start
  155.3 20.8 %shard_map.179 = (f32[1,1]{1,0:T(1,128)}, f32[6,768]{1,0:T(8,128)}, f32[6,768]{1,0:T(8,128)}, f32[6,768]{1,0:T(8,128)}, f32[2,768,768]{2,1,0:T(8,128)}, /*index=5*/f32[2,768,768]{2,1,0:T(8,128)}, f32[2,768,768]{2,1,0:T(8,128)}) custom-call(s32[2]{0:T(128)} %convert_element_type.3.used_ref, f32[8,768]{1,0:T(8,128)} %get-tuple-element.23.ssq_ref, ...), custom_call_target="tpu_custom_call" | custom-call | tf_op jit(solution)/shard_map/pallas_call | solution.py:953
  176.0 0.0 copy-done.1
  176.0 0.8 copy.22
  176.9 0.0 copy-done
  176.9 1.0 copy.23
  (1 shorter events, 0.0 us)
Async XLA Ops:
  155.2 20.8 %copy-start.1 = (bf16[384,768]{1,0:T(8,128)(2,1)S(1)}, bf16[384,768]{1,0:T(8,128)(2,1)}, u32[]{:S(2)}) copy-start(bf16[384,768]{1,0:T(8,128)(2,1)} %get-tuple-element.42) | copy-start | bytes 1769476
  155.3 21.6 %copy-start = (bf16[768,768]{1,0:T(8,128)(2,1)S(1)}, bf16[768,768]{1,0:T(8,128)(2,1)}, u32[]{:S(2)}) copy-start(bf16[768,768]{1,0:T(8,128)(2,1)} %get-tuple-element.43) | copy-start | bytes 3538948

commit v3 on v2

--- a/solution.py
+++ b/solution.py
@@ -50,13 +50,19 @@
 def kernel(
     dims,
     slot_ref,
+    sp_hbm,
+    dy_hbm,
+    x_hbm,
+    master_hbm,
+    pooled_hbm,
+    ig_hbm,
+    g_ref,
+    gs_hbm,
+    ssq_hbm,
     sp_ref,
     dy_ref,
-    x_hbm,
-    master_hbm,
     pooled_ref,
     ig_ref,
-    g_ref,
     gs_ref,
     ssq_ref,
     w,
@@ -87,6 +93,9 @@
     ar_val,
     ar_core,
     ar_chip,
+    last_val,
+    last_core,
+    last_chip,
     hx_s,
     hx_r,
     hd_s,
@@ -94,6 +103,7 @@
     il,
     sq_all,
     ld_sem,
+    st_sem,
     w_send,
     w_sib,
     w_xs,
@@ -139,6 +149,9 @@
     def dev(z_, y_, x_, c_):
         return (z_ * NY + y_, x_ * 2 + c_)
 
+    def wrap(v, n):
+        return jnp.where(v >= n, v - n, v)
+
     def remote(src, dst, ss, rs, to):
         return pltpu.make_async_remote_copy(
             src_ref=src, dst_ref=dst, send_sem=ss, recv_sem=rs, device_id=to, device_id_type=MESH
@@ -152,22 +165,55 @@
     for j in range(cap):
         pltpu.make_async_copy(master_hbm.at[j], mst.at[j], ld_sem.at[j]).start()
     pltpu.make_async_copy(x_hbm, dz, ld_sem.at[cap]).start()
+    loads = [
+        pltpu.make_async_copy(sp_hbm, sp_ref, ld_sem.at[cap + 1]),
+        pltpu.make_async_copy(dy_hbm, dy_ref, ld_sem.at[cap + 2]),
+    ]
+    for cp in loads:
+        cp.start()
+    saves = [
+        pltpu.make_async_copy(src, dst, st_sem.at[i])
+        for i, (src, dst) in enumerate(
+            ((pooled_ref, pooled_hbm), (ig_ref, ig_hbm), (gs_ref, gs_hbm), (ssq_ref, ssq_hbm))
+        )
+    ]
+
+    at_end, at_start = o_ix == own_n - 1, o_ix == 0
+    to_after = (wrap(s_ix + at_end.astype(jnp.int32), seq_n), wrap(o_ix + 1, own_n))
+    to_before = (
+        wrap(s_ix + seq_n - at_start.astype(jnp.int32), seq_n),
+        wrap(o_ix + own_n - 1, own_n),
+    )
+    chip_peers = [(ds, dx) for ds in range(seq_n) for dx in range(NX) if ds or dx]
+    plane_peers = [
+        (dy_, dx, dc) for dy_ in range(NY) for dx in range(NX) for dc in range(2) if dy_ or dx or dc
+    ]
+
+    def chip_peer(ds, dx):
+        return (wrap(s_ix + ds, seq_n), wrap(x + dx, NX) * 2 + c)
+
+    def plane_peer(dy_, dx, dc):
+        return wrap(y + dy_, NY), wrap(x + dx, NX), c + dc - 2 * c * dc
 
     barrier = pltpu.get_barrier_semaphore()
-
-    def greet(i, carry):
-        p = lax.rem(me + 1 + i, n_dev)
-        pl.semaphore_signal(
-            barrier, inc=1, device_id=(p // own_n, lax.rem(p, own_n)), device_id_type=MESH
-        )
-        return carry
-
-    lax.fori_loop(0, n_dev - 1, greet, 0)
+    crossed = [k for k in plane_peers if k[2]]
+
+    def greet(to):
+        pl.semaphore_signal(barrier, inc=1, device_id=to, device_id_type=MESH)
+
+    for k in chip_peers:
+        greet(chip_peer(*k))
+    for k in crossed:
+        py, px, pc = plane_peer(*k)
+        greet(dev(z, py, px, pc))
+    greet(to_before)
+    greet(to_after)
+    n_greet = len(chip_peers) + len(crossed) + 2
 
     for j in range(cap):
         pltpu.make_async_copy(master_hbm.at[j], mst.at[j], ld_sem.at[j]).wait()
         w[o_ix * cap + j] = mst[j].astype(BF16)
-    pl.semaphore_wait(barrier, n_dev - 1)
+    pl.semaphore_wait(barrier, n_greet)
 
     thirds = (NX, NY, NZ) == (2, 2, 4)
     QR = 64
@@ -261,33 +307,35 @@
 
     chip = s_ix * NX + x
 
+    def ar_refs(i):
+        if i == 3:
+            return last_val, last_core, last_chip
+        return ar_val.at[i], ar_core.at[i], ar_chip.at[i % ar_chip.shape[0]]
+
+    def ar_pair_copy(i):
+        val, core, _ = ar_refs(i)
+        return remote(val, core, ar_s.at[i], ar_r.at[i], sib)
+
     def ar_begin(i):
-        remote(ar_val.at[i], ar_core.at[i], ar_s.at[i], ar_r.at[i], sib).start()
-
-    def ar_chip_copy(i, k):
-        p = lax.rem(chip + 1 + k, chips)
-        ref = ar_chip.at[i % ar_chip.shape[0], chip]
-        return remote(
-            ref, ref, ar_s2.at[i], ar_r2.at[i], (p // NX, lax.rem(p, NX) * 2 + c)
-        )
+        ar_pair_copy(i).start()
 
     def ar_mid(i):
-        remote(ar_val.at[i], ar_core.at[i], ar_s.at[i], ar_r.at[i], sib).wait()
-        ar_chip[i % ar_chip.shape[0], chip] = ar_val[i] + ar_core[i]
-
-        def body(k, carry):
-            ar_chip_copy(i, k).start()
-            return carry
-
-        lax.fori_loop(0, chips - 1, body, 0)
+        ar_pair_copy(i).wait()
+        val, core, every = ar_refs(i)
+        every[chip] = val[...] + core[...]
+        for k in chip_peers:
+            ref = every.at[chip]
+            remote(ref, ref, ar_s2.at[i], ar_r2.at[i], chip_peer(*k)).start()
 
     def ar_end(i):
-        at = i % ar_chip.shape[0]
-        wait_bytes(ar_chip.at[at, pl.ds(0, chips - 1)], ar_r2.at[i])
-        wait_bytes(ar_chip.at[at, pl.ds(0, chips - 1)], ar_s2.at[i])
-        return jnp.sum(ar_chip[at], axis=0)
+        _, _, every = ar_refs(i)
+        wait_bytes(every.at[pl.ds(0, chips - 1)], ar_r2.at[i])
+        wait_bytes(every.at[pl.ds(0, chips - 1)], ar_s2.at[i])
+        return jnp.sum(every[...], axis=0)
 
     pltpu.make_async_copy(x_hbm, dz, ld_sem.at[cap]).wait()
+    for cp in loads:
+        cp.wait()
     ts = hp // 3
     total = jnp.zeros((1, ch), F32)
     square = jnp.zeros((1, ch), F32)
@@ -300,11 +348,8 @@
             total += colsum(v)
             square += colsum(v * v)
     zero_row = jnp.zeros((1, ch), F32)
-    ar_val[0] = jnp.concatenate([total, square, zero_row, zero_row], axis=0)
+    ar_val[0] = jnp.concatenate([total, square], axis=0)
     ar_begin(0)
-    before, after = lax.rem(me + n_dev - 1, n_dev), lax.rem(me + 1, n_dev)
-    to_before = (before // own_n, lax.rem(before, own_n))
-    to_after = (after // own_n, lax.rem(after, own_n))
     has_before = jnp.where(me > 0, 1.0, 0.0).astype(F32)
     has_after = jnp.where(me < n_dev - 1, 1.0, 0.0).astype(F32)
     hx_s[0] = jnp.concatenate([xf[0:1], xf[hp : hp + 1]], axis=0)
@@ -378,7 +423,6 @@
         ar_val[1, 0:1, n] = colsum(acc)
         ar_val[1, 1:2, n] = colsum(acc * acc)
 
-    ar_val[1] = jnp.zeros_like(ar_val[1])
     over_tiles(conv_tile)
     ar_begin(1)
     for i in range(nt):
@@ -476,11 +520,23 @@
     def end_copy(p):
         return remote(zs.at[p], zr.at[p, 0], z_s.at[p, 0], z_r.at[p, 0], dev(inner, y, x, c))
 
+    def direct(p):
+        return chain and p >= NMAT - 2
+
+    def direct_copy(p, k, i):
+        return remote(
+            zs.at[p, k], zr.at[p, i, k], z_s.at[p, k], z_r.at[p, 2 * i + k], dev(k + 1, y, x, c)
+        )
+
     def swap_copy(p, k):
         return remote(zs.at[p, k], zr.at[p, 1, k], z_s.at[p, 1], z_r.at[p, 1], dev(lax.rem(3 - z + NZ, NZ), y, x, c))
 
     def spread_copy(p, k, i):
-        return remote(res.at[p, k], res.at[p, k], zb_s.at[p, i], zb_r.at[p, k], dev(lax.rem(z + 1 + i, NZ), y, x, c))
+        if direct(p):
+            to = wrap(z + 1 + i, NZ)
+        else:
+            to = jnp.clip(3 - z, 0, NZ - 1) if i == 1 else jnp.where(z < 2, 0, NZ - 1)
+        return remote(res.at[p, k], res.at[p, k], zb_s.at[p, i], zb_r.at[p, k], dev(to, y, x, c))
 
     def gather_copy(p, at):
         return remote(zs.at[p], zr.at[p, at], z_s.at[p, 0], z_r.at[p, at], dev(0, y, x, c))
@@ -495,10 +551,21 @@
             for i in range((NY if k == 0 else NX) - 1):
                 v += sec[p, k, i].astype(F32)
             zs[p, k] = v.astype(BF16)
-        if chain:
+        if direct(p):
 
             @pl.when(is_outer)
             def _():
+                for k in range(2):
+                    direct_copy(p, k, z // 3).start()
+
+            @pl.when(is_inner)
+            def _():
+                direct_copy(p, 1 - my_half, 2).start()
+
+        elif chain:
+
+            @pl.when(is_outer)
+            def _():
                 end_copy(p).start()
 
         else:
@@ -508,7 +575,7 @@
                 gather_copy(p, z - 1).start()
 
     def step_pass(p):
-        if chain:
+        if chain and not direct(p):
 
             @pl.when(is_inner)
             def _():
@@ -521,9 +588,16 @@
 
             @pl.when(is_inner)
             def _():
-                swap_copy(p, my_half).wait_recv()
-                res[p, my_half] = (zs[p, my_half].astype(F32) + zr[p, 1, my_half].astype(F32)).astype(BF16)
-                for i in range(NZ - 1):
+                v = zs[p, my_half].astype(F32)
+                if direct(p):
+                    for i in range(3):
+                        direct_copy(p, my_half, i).wait_recv()
+                        v += zr[p, i, my_half].astype(F32)
+                else:
+                    swap_copy(p, my_half).wait_recv()
+                    v += zr[p, 1, my_half].astype(F32)
+                res[p, my_half] = v.astype(BF16)
+                for i in range(NZ - 1 if direct(p) else 2):
                     spread_copy(p, my_half, i).start()
 
         else:
@@ -538,6 +612,14 @@
                 for i in range(NZ - 1):
                     whole_copy(p, i).start()
 
+    def step_relay(p):
+        if chain and not direct(p):
+
+            @pl.when(is_inner)
+            def _():
+                spread_copy(p, 1 - my_half, 2).wait_recv()
+                spread_copy(p, 1 - my_half, 2).start()
+
     def step_spread(p):
         if chain:
 
@@ -546,9 +628,11 @@
                 for k in range(2):
                     spread_copy(p, k, 0).wait_recv()
 
-            @pl.when(is_inner)
-            def _():
-                spread_copy(p, 1 - my_half, 0).wait_recv()
+            if direct(p):
+
+                @pl.when(is_inner)
+                def _():
+                    spread_copy(p, 1 - my_half, 0).wait_recv()
 
         else:
 
@@ -561,13 +645,21 @@
 
             @pl.when(is_outer)
             def _():
-                end_copy(p).wait_send()
+                if direct(p):
+                    for k in range(2):
+                        direct_copy(p, k, 0).wait_send()
+                else:
+                    end_copy(p).wait_send()
 
             @pl.when(is_inner)
             def _():
-                swap_copy(p, 1 - my_half).wait_send()
+                if direct(p):
+                    direct_copy(p, 1 - my_half, 2).wait_send()
+                else:
+                    swap_copy(p, 1 - my_half).wait_send()
                 for i in range(NZ - 1):
-                    spread_copy(p, my_half, i).wait_send()
+                    half_sent = my_half if direct(p) or i < 2 else 1 - my_half
+                    spread_copy(p, half_sent, i).wait_send()
 
         else:
 
@@ -580,7 +672,6 @@
                 for i in range(NZ - 1):
                     whole_copy(p, i).wait_send()
 
-    ar_val[2] = jnp.zeros_like(ar_val[2])
     par[...] = jnp.concatenate([mu2, rstd2, zero_row, zero_row], axis=0)
 
     def mix_tile(n):
@@ -604,6 +695,7 @@
         mst[0, hp:pos, n] = p1 * dy
 
     over_tiles(pool_tile)
+    saves[0].start()
     put_gradient(0, rdt, lambda n: dl[:, n])
 
     def resid_tile(n):
@@ -614,7 +706,7 @@
         mst[0, hp:pos, n] = v1
         dz[0:hp, n] = v0.astype(BF16)
         dz[hp:pos, n] = v1.astype(BF16)
-        ar_val[2, 2:3, n] = colsum(v0) + colsum(v1)
+        last_val[3:4, n] = colsum(v0) + colsum(v1)
 
     over_tiles(resid_tile)
     step_first(0)
@@ -650,9 +742,9 @@
     ar_mid(2)
     put_gradient(1, b.at[pl.ds(0, ch)], lambda n: dz[:, n])
     step_second(0)
+    step_first(1)
     sums = ar_end(2)
-    s2, q2, e2 = sums[0:1], sums[1:2], sums[2:3]
-    step_first(1)
+    s2, q2 = sums[0:1], sums[1:2]
 
     scale2 = rstd2 * g2
 
@@ -682,21 +774,20 @@
         put_gradient(2 + t, a1t, lambda n: b[lo : lo + pos, n])
 
     tap(0)
-    step_second(1)
     tap(1)
     step_first(2)
-    step_sum(0)
+    step_second(1)
     tap(2)
     step_first(3)
+    step_sum(0)
     tap(3)
     tap(4)
+    step_second(2)
+    step_first(4)
     step_pass(0)
     step_sum(1)
-    step_second(2)
-    step_first(4)
-
-    ar_val[3] = jnp.zeros_like(ar_val[3])
-    ar_val[3, 2:3] = e1_local
+
+    last_val[2:3] = e1_local
     par[...] = jnp.concatenate([mu1, rstd1, zero_row, zero_row], axis=0)
 
     def input_tile(n):
@@ -707,32 +798,42 @@
         v = acc * d1[:, n]
         mst[1, :, n] = v
         xhat = (xf[:, n] - par[0:1, n]) * par[1:2, n]
-        ar_val[3, 0:1, n] = colsum(v)
-        ar_val[3, 1:2, n] = colsum(v * xhat)
+        last_val[0:1, n] = colsum(v)
+        last_val[1:2, n] = colsum(v * xhat)
 
     input_tile(cols(0))
     step_second(3)
     step_first(5)
     step_root(0)
     step_pass(1)
+    step_sum(2)
     for i in range(1, nt - 1):
         input_tile(cols(i))
     step_second(4)
     step_first(6)
-    step_sum(2)
+    step_relay(0)
+    step_root(1)
+    step_pass(2)
+    step_sum(3)
     input_tile(cols(nt - 1))
     ar_begin(3)
-    step_root(1)
-    step_spread(0)
+    step_second(5)
+    step_relay(1)
+    step_root(2)
+    step_pass(3)
+    step_sum(4)
     ar_mid(3)
-    step_second(5)
-    step_sum(3)
-    step_pass(2)
+    step_second(6)
+    step_relay(2)
+    step_root(3)
+    step_pass(4)
+    step_sum(5)
     sums = ar_end(3)
-    s1, q1, e1 = sums[0:1], sums[1:2], sums[2:3]
+    s1, q1, e1, e2 = sums[0:1], sums[1:2], sums[2:3], sums[3:4]
     gs_ref[...] = jnp.concatenate([q1, s1, e1, q2, s2, e2], axis=0)
+    saves[2].start()
     scale1 = rstd1 * g1
-    for i in range(3):
+    def input_rows(i):
         for k in range(2):
             lo = k * hp + i * ts
             xhat = (xf[lo : lo + ts] - mu1) * rstd1
@@ -742,50 +843,43 @@
         for j in range(ch // 128):
             ig_ref[2 * i * ts : 2 * (i + 1) * ts, j * 128 : (j + 1) * 128] = il[j].astype(BF16)
 
-    step_second(6)
-    step_sum(4)
-    step_pass(3)
-    step_root(2)
-    step_spread(1)
-    step_sum(5)
-    step_pass(4)
-    step_root(3)
-    step_spread(2)
+    input_rows(0)
+    step_relay(3)
+    step_root(4)
     step_sum(6)
-    step_pass(5)
-    step_root(4)
-    step_spread(3)
-    step_pass(6)
+    input_rows(1)
+    step_relay(4)
     step_root(5)
-    step_spread(4)
+    input_rows(2)
+    saves[1].start()
     step_root(6)
-    step_spread(5)
-    step_spread(6)
+    for p in range(NMAT):
+        step_spread(p)
 
     plane = NX * NY * 2
-    mine = (x * NY + y) * 2 + c
+
+    def plane_id(py, px, pc):
+        return (px * NY + py) * 2 + pc
+
+    mine = plane_id(y, x, c)
     for s in range(own_n * cap):
         at = jnp.int32(0)
         for p in range(NMAT):
             at = jnp.maximum(at, jnp.where(slots[ORDER[p]] == s, p, 0))
         stage[s] = res[at]
 
-    def plane_of(k):
-        p = lax.rem(mine + 1 + k, plane)
-        return p, p // (2 * NY), lax.rem(p // 2, NY), lax.rem(p, 2)
-
     def gather_send(k):
-        _, px, py, pc = plane_of(k)
+        py, px, pc = plane_peer(*plane_peers[k])
         src = stage.at[pl.ds((px * 2 + pc) * cap, cap)]
-        return remote(src, g_ref.at[:, c, x, y], g_s.at[k], g_r.at[plane - 2 - k], dev(z, py, px, pc))
+        return remote(src, g_ref.at[:, c, x, y], g_s.at[k], g_r.at[mine], dev(z, py, px, pc))
 
     def gather_recv(k):
-        _, px, py, pc = plane_of(k)
+        py, px, pc = plane_peer(*plane_peers[k])
         src = stage.at[pl.ds((px * 2 + pc) * cap, cap)]
-        return remote(src, g_ref.at[:, pc, px, py], g_s.at[k], g_r.at[k], dev(z, py, px, pc))
+        return remote(src, g_ref.at[:, pc, px, py], g_s.at[k], g_r.at[plane_id(py, px, pc)], dev(z, py, px, pc))
 
     def square_copy(k):
-        _, px, py, pc = plane_of(k)
+        py, px, pc = plane_peer(*plane_peers[k])
         ref = sq_all.at[mine]
         return remote(ref, ref, q_s.at[0], q_r.at[0], dev(z, py, px, pc))
 
@@ -810,11 +904,14 @@
     wait_bytes(sq_all.at[pl.ds(0, plane - 1)], q_r.at[0])
     wait_bytes(sq_all.at[pl.ds(0, plane - 1)], q_s.at[0])
     ssq_ref[...] = jnp.sum(sq_all[...], axis=0)
+    saves[3].start()
     for k in range(plane - 1):
         gather_send(k).wait_send()
     for k in range(plane - 1):
         gather_recv(k).wait_recv()
     keep.wait()
+    for cp in saves:
+        cp.wait()
 
 
 def adam(grads, first_old, second_old):
@@ -827,12 +924,12 @@
 
 
 def optimizer_kernel(
-    used_ref,
-    ssq_ref,
-    gs_ref,
-    sp_ref,
-    sf_ref,
-    ss_ref,
+    slot_ref,
+    ssq_hbm,
+    gs_hbm,
+    sp_hbm,
+    sf_hbm,
+    ss_hbm,
     g_hbm,
     left_hbm,
     right_hbm,
@@ -840,9 +937,9 @@
     second_hbm,
     master_hbm,
     norm_ref,
-    nsp_ref,
-    nsf_ref,
-    nss_ref,
+    nsp_hbm,
+    nsf_hbm,
+    nss_hbm,
     nmaster_hbm,
     nfirst_hbm,
     nsecond_hbm,
@@ -857,8 +954,14 @@
     right_low,
     mid,
     turn,
+    ssq,
+    gs_all,
+    sp,
+    sf,
+    ss,
     in_sem,
     out_sem,
+    small_sem,
 ):
     cap, ch, _ = g.shape
     nt = ch // TILE
@@ -869,25 +972,45 @@
         return pltpu.make_async_copy(sources[i].at[j], places[i].at[j], in_sem.at[i, j])
 
     def save(i, j):
-        src = (first, second, master)[i]
-        dst = (nfirst_hbm, nsecond_hbm, nmaster_hbm)[i]
+        src = (first, second)[i]
+        dst = (nfirst_hbm, nsecond_hbm)[i]
         return pltpu.make_async_copy(src.at[j], dst.at[j], out_sem.at[i, j])
 
-    for j in range(cap):
-        for i in range(6):
-            load(i, j).start()
-
-    gs = gs_ref[...]
-    norm = jnp.sqrt(
-        jnp.sum(jnp.sum(ssq_ref[...], axis=0, keepdims=True), axis=1, keepdims=True)
-        + jnp.sum(jnp.sum(gs * gs, axis=0, keepdims=True), axis=1, keepdims=True)
-    )
-    norm_ref[...] = norm
-    factor = jnp.minimum(1.0, CLIP_RATIO * ch * math.sqrt(NMAT) / (norm + 1e-06))
-    small_first, small_second, small_dir = adam(gs * factor, sf_ref[...], ss_ref[...])
-    nsf_ref[...] = small_first
-    nss_ref[...] = small_second
-    nsp_ref[...] = sp_ref[...] - SMALL_RATE * (small_dir + DECAY_RATE * sp_ref[...])
+    def save_rows(j, i):
+        at = pl.ds(i * TILE, TILE)
+        return pltpu.make_async_copy(master.at[j, at], nmaster_hbm.at[j, at], out_sem.at[2 + i, j])
+
+    for i in range(3):
+        load(i, 0).start()
+
+    smalls = (ssq, gs_all, sp, sf, ss)
+
+    def small_load(i):
+        return pltpu.make_async_copy((ssq_hbm, gs_hbm, sp_hbm, sf_hbm, ss_hbm)[i], smalls[i], small_sem.at[i])
+
+    def small_save(i):
+        return pltpu.make_async_copy(smalls[2 + i], (nsp_hbm, nsf_hbm, nss_hbm)[i], small_sem.at[i])
+
+    for i in range(5):
+        small_load(i).start()
+
+    def small_update():
+        for i in range(5):
+            small_load(i).wait()
+        gs = gs_all[...]
+        norm = jnp.sqrt(
+            jnp.sum(jnp.sum(ssq[...], axis=0, keepdims=True), axis=1, keepdims=True)
+            + jnp.sum(jnp.sum(gs * gs, axis=0, keepdims=True), axis=1, keepdims=True)
+        )
+        norm_ref[...] = norm
+        factor = jnp.minimum(1.0, CLIP_RATIO * ch * math.sqrt(NMAT) / (norm + 1e-06))
+        small_first, small_second, small_dir = adam(gs * factor, sf[...], ss[...])
+        sp[...] = sp[...] - SMALL_RATE * (small_dir + DECAY_RATE * sp[...])
+        sf[...] = small_first
+        ss[...] = small_second
+        for i in range(3):
+            small_save(i).start()
+        return factor
 
     def over_tiles(fn):
         def body(n, carry):
@@ -897,21 +1020,33 @@
         lax.fori_loop(0, nt, body, 0)
 
     for j in range(cap):
-        used = used_ref[j] > 0
+        slot = lax.axis_index("own") * cap + j
+        used = slot_ref[0] == slot
+        for k in range(1, NMAT):
+            used = jnp.logical_or(used, slot_ref[k] == slot)
         load(0, j).wait()
         load(1, j).wait()
+        for i in range(3, 6):
+            load(i, j).start()
         right_low[...] = right[j].astype(BF16)
 
         def mid_tile(n):
             mid[:, n] = mm(g[j], right_low[:, n]).astype(BF16)
 
         over_tiles(mid_tile)
+        if j == 0:
+            factor = small_update()
         load(2, j).wait()
+        if j + 1 < cap:
+            load(0, j + 1).start()
+            load(1, j + 1).start()
         left_low[...] = left[j].astype(BF16)
         for i in range(nt):
             left_t[i * TILE : (i + 1) * TILE, :] = left_low[:, i * TILE : (i + 1) * TILE].T
         load(3, j).wait()
         load(4, j).wait()
+        if j + 1 < cap:
+            load(2, j + 1).start()
 
         def moment_tile(n):
             grads = factor * mm(left_t[...], mid[:, n])
@@ -931,20 +1066,23 @@
         over_tiles(back_tile)
         load(5, j).wait()
 
-        def master_tile(n):
-            old = master[j, :, n]
-            step = mm_t(mid[...], right_low[n, :]) + DECAY_RATE * old
-            master[j, :, n] = jnp.where(used, old - LEARN_RATE * step, old)
-
-        over_tiles(master_tile)
-        save(2, j).start()
+        for i in range(nt):
+            at = pl.ds(i * TILE, TILE)
+            old = master[j, at, :]
+            step = mm_t(mid[at, :], right_low[...]) + DECAY_RATE * old
+            master[j, at, :] = jnp.where(used, old - LEARN_RATE * step, old)
+            save_rows(j, i).start()
+    for i in range(3):
+        small_save(i).wait()
     for j in range(cap):
-        for i in range(3):
+        for i in range(2):
             save(i, j).wait()
-
-
-def optimizer(used, squares, small_grad, small_params, small_first, small_second, owned, left, right, first, second, master):
-    cap, ch, _ = master.shape
+        for i in range(nt):
+            save_rows(j, i).wait()
+
+
+def optimizer(slots, squares, small_grad, small_params, small_first, small_second, *large):
+    cap, ch, _ = large[5].shape
     vm, dma = pltpu.VMEM, pltpu.SemaphoreType.DMA
     in_vmem = pl.BlockSpec(memory_space=pltpu.VMEM)
     anywhere = pl.BlockSpec(memory_space=pl.ANY)
@@ -952,15 +1090,25 @@
     small = jax.ShapeDtypeStruct((6, ch), F32)
     return pl.pallas_call(
         optimizer_kernel,
-        out_shape=(jax.ShapeDtypeStruct((1, 1), F32), small, small, small, big, big, big),
-        in_specs=[pl.BlockSpec(memory_space=pltpu.SMEM)] + [in_vmem] * 5 + [anywhere] * 6,
-        out_specs=(in_vmem,) * 4 + (anywhere,) * 3,
+        out_shape=(
+            jax.ShapeDtypeStruct((1, 1), F32),
+            small,
+            small,
+            small,
+            big,
+            big,
+            big,
+        ),
+        in_specs=[pl.BlockSpec(memory_space=pltpu.SMEM)] + [anywhere] * 11,
+        out_specs=(in_vmem,) + (anywhere,) * 6,
         scratch_shapes=[vm((cap, ch, ch), BF16)]
         + [vm((cap, ch, ch), F32)] * 5
         + [vm((ch, ch), BF16)] * 5
-        + [dma((6, cap)), dma((3, cap))],
+        + [vm((8, ch), F32)]
+        + [vm((6, ch), F32)] * 4
+        + [dma((6, cap)), dma((2 + ch // TILE, cap)), dma((5,))],
         compiler_params=pltpu.CompilerParams(vmem_limit_bytes=60 * 2**20),
-    )(used, squares, small_grad, small_params, small_first, small_second, owned, left, right, first, second, master)
+    )(slots, squares, small_grad, small_params, small_first, small_second, *large)
 
 
 def block_and_grads(inputs, cotangent, small_params, slot_of_matrix, master):
@@ -981,6 +1129,12 @@
     dma = pltpu.SemaphoreType.DMA
     vm = pltpu.VMEM
     scratch = [
+        vm((6, ch), F32),
+        vm((hp, ch), BF16),
+        vm((hp, ch), BF16),
+        vm((pos, ch), BF16),
+        vm((6, ch), F32),
+        vm((8, ch), F32),
         vm((slots, ch, ch), BF16),
         vm((max(cap, 2), ch, ch), F32),
         vm((pos, ch), F32),
@@ -1001,21 +1155,25 @@
         vm((NMAT, halves, nx, ny, rh, ch), BF16),
         vm((NMAT, halves, nn - 1, nn, rh, ch), BF16),
         vm((NMAT, halves, nn - 1, rh, ch), BF16),
-        vm((NMAT, 2 if nz == 4 else nz - 1, halves, rh, ch), BF16),
+        vm((NMAT, nz - 1, halves, rh, ch), BF16),
         vm((NMAT, halves, rh, ch), BF16),
         vm((NMAT, halves, rh, ch), BF16),
         vm((slots, halves, rh, ch), BF16),
         vm((4, ch), F32),
-        vm((4, 4, ch), F32),
-        vm((4, 4, ch), F32),
-        vm((4 if chips <= 16 else 2, chips, 4, ch), F32),
+        vm((3, 2, ch), F32),
+        vm((3, 2, ch), F32),
+        vm((3 if chips <= 16 else 2, chips, 2, ch), F32),
+        vm((4, ch), F32),
+        vm((4, ch), F32),
+        vm((chips, 4, ch), F32),
         vm((2, 2, ch), F32),
         vm((2, 2, ch), F32),
         vm((2, 8, ch), F32),
         vm((2, 8, ch), F32),
         vm((ch // 128, hp // 3 * 2, 128), F32),
         vm((plane, 8, ch), F32),
-        dma((cap + 1,)),
+        dma((cap + 3,)),
+        dma((4,)),
         dma((1,)),
         dma((1,)),
         dma((cap * 4,)),
@@ -1035,16 +1193,15 @@
         dma((NMAT, halves, nn - 1)),
         dma((NMAT, halves, nn - 1)),
         dma((NMAT, 2)),
-        dma((NMAT, max(2, nz - 1))),
+        dma((NMAT, 2 * nz - 2)),
         dma((NMAT, nz - 1)),
         dma((NMAT, 2)),
         dma((plane - 1,)),
-        dma((plane - 1,)),
+        dma((plane,)),
         dma((1,)),
         dma((1,)),
         dma((1,)),
     ]
-    in_vmem = pl.BlockSpec(memory_space=pltpu.VMEM)
     anywhere = pl.BlockSpec(memory_space=pl.ANY)
     return pl.pallas_call(
         functools.partial(kernel, (nx, ny, nz, cap, pos * seq_n * own_n)),
@@ -1055,8 +1212,8 @@
             jax.ShapeDtypeStruct((6, ch), F32),
             jax.ShapeDtypeStruct((8, ch), F32),
         ),
-        in_specs=[pl.BlockSpec(memory_space=pltpu.SMEM), in_vmem, in_vmem, anywhere, anywhere],
-        out_specs=(in_vmem, in_vmem, anywhere, in_vmem, in_vmem),
+        in_specs=[pl.BlockSpec(memory_space=pltpu.SMEM)] + [anywhere] * 4,
+        out_specs=(anywhere,) * 5,
         scratch_shapes=scratch,
         compiler_params=pltpu.CompilerParams(
             collective_id=0, has_side_effects=True, vmem_limit_bytes=63 * 2**20
@@ -1078,14 +1235,19 @@
     right_basis,
 ):
     cap, ch = master.shape[0], master.shape[2]
-    own_n = lax.axis_size("own")
     pooled, input_grad, owned, small_grad, squares = block_and_grads(
         inputs, cotangent, small_params, slot_of_matrix, master
     )
-    slot_ids = lax.axis_index("own") * cap + jnp.arange(cap, dtype=jnp.int32)
-    used = jnp.any(slot_ids[:, None] == slot_of_matrix[None, :], axis=1).astype(jnp.int32)
-    grad_norm, new_small, small_first_new, small_second_new, new_master, new_first, new_second = optimizer(
-        used,
+    (
+        grad_norm,
+        new_small,
+        small_first_new,
+        small_second_new,
+        new_master,
+        new_first,
+        new_second,
+    ) = optimizer(
+        slot_of_matrix,
         squares,
         small_grad,
         small_params,

time: 178 us -> 168 us (0.944)
  Pallas kernels: 174 us -> 166 us
    pallas_call x1, Pallas kernels: 153 us -> 145 us  [block_and_grads(): pl.pallas_call(functools.partial(kernel, (nx, ny, nz, cap, pos * seq_n *...]
where the time goes in v3:
time: 168 us
  Pallas kernels  166 us (99%)
  local copies, waits for them, and re-layouts  1.84 us (1%)
    pallas_call x1, Pallas kernels, block_and_grads(): pl.pallas_call(functools.partial(kernel, (nx, ny, nz, cap, pos * seq_n *...  145 us
    pallas_call x1, Pallas kernels, optimizer(): pl.pallas_call(optimizer_kernel, out_shape=(jax.ShapeDtypeStruct((1, 1),...  20.4 us

profile of v3, /device:TPU:0, one launch (start us, length us, event | category | flops | bytes accessed | tf_op | source)
XLA Modules:
  0.0 168.0 jit_solution(3307058690495844464)
XLA Ops:
  0.6 145.1 %shard_map.178 = (bf16[384,768]{1,0:T(8,128)(2,1)}, bf16[768,768]{1,0:T(8,128)(2,1)}, bf16[2,2,2,2,2,48,768]{6,5,4,3,2,1,0:T(8,128)(2,1)}, f32[6,768]{1,0:T(8,128)}, f32[8,768]{1,0:T(8,128)}) custom-call(s32[7]{0:T(128)} %slot_ref.3, f32[6,768]{1,0:T(8,128)} %sp_hbm.3, bf16[384,768]{1,0:T(8,128)(2,1)} %dy_hbm.1, bf16[768,768]{1,0:T(8,128)(2,1)} %x_hbm.1, ...), custom_call_target="tpu_custom_call" | custom-call | tf_op jit(solution)/shard_map/pallas_call | solution.py:1206
  145.8 0.0 copy-start.1
  145.8 0.0 copy-start
  145.8 20.4 %shard_map.179 = (f32[1,1]{1,0:T(1,128)}, f32[6,768]{1,0:T(8,128)}, f32[6,768]{1,0:T(8,128)}, f32[6,768]{1,0:T(8,128)}, f32[2,768,768]{2,1,0:T(8,128)}, /*index=5*/f32[2,768,768]{2,1,0:T(8,128)}, f32[2,768,768]{2,1,0:T(8,128)}) custom-call(s32[7]{0:T(128)} %slot_ref.3, f32[8,768]{1,0:T(8,128)} %get-tuple-element.23.ssq_hbm, ...), custom_call_target="tpu_custom_call" | custom-call | tf_op jit(solution)/shard_map/pallas_call | solution.py:1091
  166.2 0.0 copy-done.1
  166.2 0.8 copy.22
  167.0 0.0 copy-done
  167.0 1.0 copy.23
Async XLA Ops:
  145.8 20.4 %copy-start.1 = (bf16[384,768]{1,0:T(8,128)(2,1)S(1)}, bf16[384,768]{1,0:T(8,128)(2,1)}, u32[]{:S(2)}) copy-start(bf16[384,768]{1,0:T(8,128)(2,1)} %get-tuple-element.42) | copy-start | bytes 1769476
  145.8 21.3 %copy-start = (bf16[768,768]{1,0:T(8,128)(2,1)S(1)}, bf16[768,768]{1,0:T(8,128)(2,1)}, u32[]{:S(2)}) copy-start(bf16[768,768]{1,0:T(8,128)(2,1)} %get-tuple-element.43) | copy-start | bytes 3538948

commit v4 on v3

--- a/solution.py
+++ b/solution.py
@@ -128,6 +128,8 @@
     zb_r,
     g_s,
     g_r,
+    p_s,
+    p_r,
     q_s,
     q_r,
     g_l,
@@ -405,14 +407,11 @@
     slots = [slot_ref[k] for k in range(NMAT)]
 
     def cols(n):
-        return pl.ds(pl.multiple_of(n * TILE, TILE), TILE)
+        return slice(n * TILE, (n + 1) * TILE)
 
     def over_tiles(fn):
-        def body(n, carry):
+        for n in range(nt):
             fn(cols(n))
-            return carry
-
-        lax.fori_loop(0, nt, body, 0)
 
     def conv_tile(n):
         acc = mm(b[0:pos, :], w[slots[0], :, n])
@@ -883,7 +882,31 @@
         ref = sq_all.at[mine]
         return remote(ref, ref, q_s.at[0], q_r.at[0], dev(z, py, px, pc))
 
-    for k in range(plane - 1):
+    paired = (NX, NY) == (2, 2) and NZ % 2 == 0 and halves == 2
+    diagonal = [k for k, (dy_, dx, _) in enumerate(plane_peers) if paired and dy_ and dx]
+    later = [k for k, (dy_, dx, _) in enumerate(plane_peers) if paired and dx and not dy_]
+    direct_now = [k for k in range(plane - 1) if k not in diagonal and k not in later]
+    odd = lax.rem(z, 2)
+
+    def half_send(k):
+        py, px, pc = plane_peer(*plane_peers[k])
+        src = stage.at[pl.ds((px * 2 + pc) * cap, cap), odd]
+        return remote(src, g_ref.at[:, c, x, y, odd], g_s.at[k], g_r.at[mine], dev(z, py, px, pc))
+
+    def half_recv(k):
+        py, px, pc = plane_peer(*plane_peers[k])
+        src = stage.at[pl.ds((px * 2 + pc) * cap, cap), odd]
+        at = plane_id(py, px, pc)
+        return remote(src, g_ref.at[:, pc, px, py, odd], g_s.at[k], g_r.at[at], dev(z, py, px, pc))
+
+    def hand_over(k, part):
+        py, px, pc = plane_peer(*plane_peers[k])
+        ref = g_ref.at[:, pc, px, py, part]
+        return remote(ref, ref, p_s.at[pc], p_r.at[pc], dev(z + 1 - 2 * odd, y, x, c))
+
+    for k in diagonal:
+        half_send(k).start()
+    for k in direct_now:
         gather_send(k).start()
     keep = pltpu.make_async_copy(
         stage.at[pl.ds(o_ix * cap, cap)], g_ref.at[:, c, x, y], g_l.at[0]
@@ -899,16 +922,26 @@
     sq_all[mine] = sq
     for k in range(plane - 1):
         square_copy(k).start()
+    for k in diagonal:
+        half_send(k).wait_send()
+    for k in later:
+        gather_send(k).start()
     for p in range(NMAT):
         step_done(p)
+    for k in diagonal:
+        half_recv(k).wait_recv()
+        hand_over(k, odd).start()
     wait_bytes(sq_all.at[pl.ds(0, plane - 1)], q_r.at[0])
     wait_bytes(sq_all.at[pl.ds(0, plane - 1)], q_s.at[0])
     ssq_ref[...] = jnp.sum(sq_all[...], axis=0)
     saves[3].start()
-    for k in range(plane - 1):
+    for k in direct_now + later:
         gather_send(k).wait_send()
-    for k in range(plane - 1):
+    for k in direct_now + later:
         gather_recv(k).wait_recv()
+    for k in diagonal:
+        hand_over(k, odd).wait_send()
+        hand_over(k, 1 - odd).wait_recv()
     keep.wait()
     for cp in saves:
         cp.wait()
@@ -1198,6 +1231,8 @@
         dma((NMAT, 2)),
         dma((plane - 1,)),
         dma((plane,)),
+        dma((2,)),
+        dma((2,)),
         dma((1,)),
         dma((1,)),
         dma((1,)),

time: 168 us -> 160 us (0.952)
  Pallas kernels: 166 us -> 157 us
    pallas_call x1, Pallas kernels: 145 us -> 137 us  [block_and_grads(): pl.pallas_call(functools.partial(kernel, (nx, ny, nz, cap, pos * seq_n *...]
where the time goes in v4:
time: 160 us; the launch traced here: 159 us
  Pallas kernels  157 us (98%)
  local copies, waits for them, and re-layouts  1.84 us (1%)
    pallas_call x1, Pallas kernels, block_and_grads(): pl.pallas_call(functools.partial(kernel, (nx, ny, nz, cap, pos * seq_n *...  137 us
    pallas_call x1, Pallas kernels, optimizer(): pl.pallas_call(optimizer_kernel, out_shape=(jax.ShapeDtypeStruct((1, 1),...  20.4 us

profile of v4, /device:TPU:0, one launch (start us, length us, event | category | flops | bytes accessed | tf_op | source)
XLA Modules:
  0.0 159.5 jit_solution(15664110638073494733)
XLA Ops:
  0.6 136.6 %shard_map.178 = (bf16[384,768]{1,0:T(8,128)(2,1)}, bf16[768,768]{1,0:T(8,128)(2,1)}, bf16[2,2,2,2,2,48,768]{6,5,4,3,2,1,0:T(8,128)(2,1)}, f32[6,768]{1,0:T(8,128)}, f32[8,768]{1,0:T(8,128)}) custom-call(s32[7]{0:T(128)} %slot_ref.3, f32[6,768]{1,0:T(8,128)} %sp_hbm.3, bf16[384,768]{1,0:T(8,128)(2,1)} %dy_hbm.1, bf16[768,768]{1,0:T(8,128)(2,1)} %x_hbm.1, ...), custom_call_target="tpu_custom_call" | custom-call | tf_op jit(solution)/shard_map/pallas_call | solution.py:1241
  137.2 0.0 copy-start.1
  137.2 0.0 copy-start
  137.2 20.4 %shard_map.179 = (f32[1,1]{1,0:T(1,128)}, f32[6,768]{1,0:T(8,128)}, f32[6,768]{1,0:T(8,128)}, f32[6,768]{1,0:T(8,128)}, f32[2,768,768]{2,1,0:T(8,128)}, /*index=5*/f32[2,768,768]{2,1,0:T(8,128)}, f32[2,768,768]{2,1,0:T(8,128)}) custom-call(s32[7]{0:T(128)} %slot_ref.3, f32[8,768]{1,0:T(8,128)} %get-tuple-element.23.ssq_hbm, ...), custom_call_target="tpu_custom_call" | custom-call | tf_op jit(solution)/shard_map/pallas_call | solution.py:1124
  157.7 0.0 copy-done.1
  157.7 0.8 copy.22
  158.5 0.0 copy-done
  158.5 1.0 copy.23
Async XLA Ops:
  137.2 20.4 %copy-start.1 = (bf16[384,768]{1,0:T(8,128)(2,1)S(1)}, bf16[384,768]{1,0:T(8,128)(2,1)}, u32[]{:S(2)}) copy-start(bf16[384,768]{1,0:T(8,128)(2,1)} %get-tuple-element.42) | copy-start | bytes 1769476
  137.2 21.3 %copy-start = (bf16[768,768]{1,0:T(8,128)(2,1)S(1)}, bf16[768,768]{1,0:T(8,128)(2,1)}, u32[]{:S(2)}) copy-start(bf16[768,768]{1,0:T(8,128)(2,1)} %get-tuple-element.43) | copy-start | bytes 3538948
